TPU v7x, 512 devices: a whole 4x8x8 slice. The times are simulated.
512 devices in a mesh: lon: 32 (over x, z_lo, core), ch: 16 (over z_hi, y).
Axes of the slice: x: 4, y: 8, z: 8 (z_hi: 2, z_lo: 4; z = z_hi * 4 + z_lo), core: 2. Of those that a mesh axis runs over, the one named last changes fastest.
Arguments:
- fields: bfloat16 [2, 512, 1440, 128], P(None, 'ch', 'lon'), may hold values from -6 to 6
- zonal_taps: bfloat16 [512, 181], P('ch'), may hold values from -0.4375 to 0.4375
- conv_weight: bfloat16 [512, 16, 3, 3], P('ch'), may hold values from -0.5 to 0.5
- mix_weight: bfloat16 [512, 512], P('ch'), may hold values from -0.25 to 0.25
Outputs:
- updated: bfloat16 [2, 512, 1440, 128], P(None, 'ch', 'lon')
All inputs are finite; a program needn't handle non-finite values.
Results may differ from a plain program's by a relative error of at most 0.009.
Values may be sent and summed in bfloat16 or wider, within the bound.
No kernel may reach another device: no remote copies, remote signals or barrier semaphores. Data moves between devices by JAX's collectives and lax.ppermute only.
A program may use at most 64 MiB of HBM per device.

v0:
```python
import jax
import jax.numpy as jnp
from jax import lax
from jax.sharding import PartitionSpec as P

GROUP_WIDTH = 16
GROUP_DILATION = 4


def passed_along(block, axis, distance):
    devices = range(lax.axis_size(axis))
    route = [((i - distance) % len(devices), i) for i in devices]
    return lax.ppermute(block, axis, route)


def extended(block, sides, width):
    for axis, dim in sides:
        count = lax.axis_size(axis)
        forward = [(i, i + 1) for i in range(count - 1)]
        forward.append((count - 1, 0))
        backward = [(target, source) for source, target in forward]
        low = lax.ppermute(
            lax.slice_in_dim(block, block.shape[dim] - width, None, axis=dim), axis, forward
        )
        high = lax.ppermute(lax.slice_in_dim(block, 0, width, axis=dim), axis, backward)
        block = jnp.concatenate([low, block, high], axis=dim)
    return block


def per_device(fields, zonal_taps, conv_weight, mix_weight):
    ensemble_members, chans, field_width, row_block = fields.shape
    sides = {}
    for offset in (1, 2, -1, -2):
        sides[offset] = passed_along(fields, "lon", offset)
    window = jnp.concatenate([sides[2], sides[1], fields, sides[-1], sides[-2]], axis=2)
    offsets = jnp.arange(5 * field_width)[:, None] - jnp.arange(field_width)[None, :]
    inside = (offsets >= 0) & (offsets <= 4 * field_width)
    clipped = jnp.clip(offsets, 0, 4 * field_width)
    toeplitz = jnp.where(inside[None], zonal_taps[:, clipped], jnp.zeros((), jnp.bfloat16))
    zonal_output = jnp.einsum(
        "mcjr,cjl->mclr", window, toeplitz, preferred_element_type=jnp.float32
    ).astype(jnp.bfloat16)
    halo_padded = extended(zonal_output, (("lon", 2),), GROUP_DILATION)
    padded_field = jnp.pad(halo_padded, ((0, 0), (0, 0), (0, 0), (GROUP_DILATION, GROUP_DILATION)))
    local_groups = chans // GROUP_WIDTH
    grouped_output = padded_field.reshape(
        ensemble_members,
        local_groups,
        GROUP_WIDTH,
        field_width + 2 * GROUP_DILATION,
        row_block + 2 * GROUP_DILATION,
    )
    kernel = conv_weight.reshape(local_groups, GROUP_WIDTH, GROUP_WIDTH, 3, 3)
    summed = jnp.zeros(
        (ensemble_members, local_groups, GROUP_WIDTH, field_width, row_block), jnp.float32
    )
    for latitude_taps in range(3):
        for longitude_taps in range(3):
            section = grouped_output[
                :,
                :,
                :,
                longitude_taps * GROUP_DILATION : longitude_taps * GROUP_DILATION + field_width,
                latitude_taps * GROUP_DILATION : latitude_taps * GROUP_DILATION + row_block,
            ]
            summed = summed + jnp.einsum(
                "goi,mgilr->mgolr",
                kernel[:, :, :, latitude_taps, longitude_taps],
                section,
                preferred_element_type=jnp.float32,
            )
    hidden = jax.nn.gelu(
        summed.reshape(ensemble_members, chans, field_width, row_block), approximate=False
    ).astype(jnp.bfloat16)
    mixed = jnp.einsum(
        "oi,milr->molr",
        mix_weight,
        lax.all_gather(hidden, "ch", axis=1, tiled=True),
        preferred_element_type=jnp.float32,
    ).astype(jnp.bfloat16)
    return (fields.astype(jnp.float32) + mixed.astype(jnp.float32)).astype(jnp.bfloat16)


def solution(mesh):
    return jax.shard_map(
        per_device,
        mesh=mesh,
        in_specs=(
            P(None, "ch", "lon", None),
            P("ch", None),
            P("ch", None, None, None),
            P("ch", None),
        ),
        out_specs=P(None, "ch", "lon", None),
        check_vma=False,
    )
```

profile of v0, /device:TPU:6, one launch (start us, length us, event | category | flops | bytes accessed | tf_op | source)
XLA Modules:
  0.0 417.7 jit_solution(14940785825516747727)
XLA Ops:
  6.5 7.7 %collective-permute-start.2 = (bf16[2,32,45,128]{3,1,2,0:T(8,128)(2,1)}, bf16[2,32,45,128]{3,1,2,0:T(8,128)(2,1)}, u32[]{:S(2)}, u32[]{:S(2)}) collective-permute-start(bf16[2,32,45,128]{3,1,2,0:T(8,128)(2,1)} %param.4), channel_id=1, source_target_pairs={{16,0},{32,16},{48,32},{64,48},{80,64},{96,80},{112,96},{128,112},... | collective-permute-start | bytes 2211848 | tf_op jit(solution)/shard_map/ppermute | solution.py:13
  14.3 1.9 collective-permute-start.1
  16.2 1.9 collective-permute-start
  18.1 6.6 %collective-permute-start.3 = (bf16[2,32,45,128]{3,1,2,0:T(8,128)(2,1)}, bf16[2,32,45,128]{3,1,2,0:T(8,128)(2,1)}, u32[]{:S(2)}, u32[]{:S(2)}) collective-permute-start(bf16[2,32,45,128]{3,1,2,0:T(8,128)(2,1)} %param.4), channel_id=1, source_target_pairs={{32,0},{48,16},{64,32},{80,48},{96,64},{112,80},{128,96},{144,112}... | collective-permute-start | bytes 2211848 | tf_op jit(solution)/shard_map/ppermute | solution.py:13
  24.8 1.4 copy.46
  26.6 30.4 %gather_fusion = bf16[10125,32]{1,0:T(8,128)(2,1)S(1)} fusion(bf16[32,181]{0,1:T(8,128)(2,1)S(1)} %copy.42, s32[10240]{0:T(1024)S(1)} %pad_clamp_fusion), kind=kCustom, calls=%fused_computation | custom fusion | bytes 1336500 | tf_op jit(solution)/shard_map/gather | solution.py:39
  57.0 2.8 copy.43
  59.8 2.7 reshape.62
  62.6 1.4 copy.47
  64.0 2.3 copy.45
  66.3 2.3 copy.44
  68.7 2.3 copy.48
  71.0 32.4 %concatenate.6 = bf16[2,32,225,128]{3,2,0,1:T(8,128)(2,1)} concatenate(bf16[2,32,45,128]{3,2,0,1:T(8,128)(2,1)} %copy.44, bf16[2,32,45,128]{3,2,0,1:T(8,128)(2,1)} %copy.45, bf16[2,32,45,128]{3,2,0,1:T(8,128)(2,1)S(1)} %copy.46, bf16[2,32,45,128]{3,2,0,1:T(8,128)(2,1)S(1)} %copy.47, bf16[2,32,45,128]{3,2,0,1:T(8,128)(2,1)} %copy.48), dimensions={2} | concatenate | bytes 7372800 | tf_op jit(solution)/shard_map/concatenate | solution.py:35
  103.4 2.9 fusion.31
  106.4 1.9 collective-permute-start.4
  108.3 6.5 %collective-permute-start.5 = (bf16[2,32,4,128]{3,2,0,1:T(4,128)(2,1)S(1)}, bf16[2,32,4,128]{3,2,0,1:T(4,128)(2,1)S(1)}, u32[]{:S(2)}, u32[]{:S(2)}) collective-permute-start(bf16[2,32,4,128]{3,2,0,1:T(4,128)(2,1)S(1)} %get-tuple-element.17), channel_id=1, source_target_pairs={{16,0},{32,16},{48,32},{64,48},{80,64},{96,80},{112,96},{128,112},... | collective-permute-start | bytes 196616 | tf_op jit(solution)/shard_map/ppermute | solution.py:25
  114.9 1.6 collective-permute-done.5
  116.5 1.4 fusion.9
  118.0 2.2 fusion.57
  120.2 0.4 fusion.36
  120.5 0.4 fusion.38
  120.9 0.4 fusion.40
  121.2 0.4 fusion.42
  121.6 0.4 fusion.44
  122.0 0.4 fusion.46
  122.3 0.4 fusion.48
  122.7 0.4 fusion.50
  123.1 0.8 multiply_bitcast_fusion.1
  124.1 0.2 copy.61
  124.4 4.0 fusion.12
  128.4 275.1 %all-gather.2.cloned.1.call-done = bf16[2,512,45,128]{3,1,2,0:T(8,128)(2,1)} async-done(((bf16[2,32,45,128]{3,1,2,0:T(8,128)(2,1)}), bf16[2,512,45,128]{3,1,2,0:T(8,128)(2,1)}) %all-gather.2.cloned.1.call-update) | async-done | bytes 11796496 | tf_op jit(solution)/shard_map/all_gather | solution.py:78
  403.5 7.3 %fusion.13 = bf16[2,32,45,128]{3,1,2,0:T(8,128)(2,1)} fusion(bf16[2,32,45,128]{3,1,2,0:T(8,128)(2,1)S(1)} %copy-done.1, bf16[2,512,45,128]{3,1,2,0:T(8,128)(2,1)} %all-gather.2.cloned.1.call-done, bf16[32,512]{1,0:T(8,128)(2,1)S(1)} %copy-done), kind=kOutput, calls=%fused_computation.18 | convolution fusion | flops 379330560 | bytes 13303808 | tf_op jit(solution)/shard_map/oi,milr->molr/dot_general | solution.py:75
  (23 shorter events, 0.8 us)
Async XLA Ops:
  6.5 396.9 %copy-start = (bf16[32,512]{1,0:T(8,128)(2,1)S(1)}, bf16[32,512]{1,0:T(8,128)(2,1)}, u32[]{:S(2)}) copy-start(bf16[32,512]{1,0:T(8,128)(2,1)} %param.7) | copy-start | bytes 98308
  6.5 19.7 %copy-start.3 = (bf16[32,181]{1,0:T(8,128)(2,1)S(1)}, bf16[32,181]{1,0:T(8,128)(2,1)}, u32[]{:S(2)}) copy-start(bf16[32,181]{1,0:T(8,128)(2,1)} %param.5) | copy-start | bytes 34756
  6.5 396.9 %all-gather.2.cloned.1.call-start = ((), (), s32[]{:S(2)}) async-start(), calls=%async_computation | async-start | bytes 12533760 | tf_op jit(solution)/shard_map/all_gather | solution.py:78
  6.5 56.0 %collective-permute-start.2 = (bf16[2,32,45,128]{3,1,2,0:T(8,128)(2,1)}, bf16[2,32,45,128]{3,1,2,0:T(8,128)(2,1)}, u32[]{:S(2)}, u32[]{:S(2)}) collective-permute-start(bf16[2,32,45,128]{3,1,2,0:T(8,128)(2,1)} %param.4), channel_id=1, source_target_pairs={{16,0},{32,16},{48,32},{64,48},{80,64},{96,80},{112,96},{128,112},... | collective-permute-start | bytes 2211848 | tf_op jit(solution)/shard_map/ppermute | solution.py:13
  14.3 49.7 %collective-permute-start.1 = (bf16[2,32,45,128]{3,1,2,0:T(8,128)(2,1)}, bf16[2,32,45,128]{3,1,2,0:T(8,128)(2,1)}, u32[]{:S(2)}, u32[]{:S(2)}) collective-permute-start(bf16[2,32,45,128]{3,1,2,0:T(8,128)(2,1)} %param.4), channel_id=1, source_target_pairs={{496,0},{0,16},{16,32},{32,48},{48,64},{64,80},{80,96},{96,112},{1... | collective-permute-start | bytes 2211848 | tf_op jit(solution)/shard_map/ppermute | solution.py:13
  16.2 50.1 %collective-permute-start = (bf16[2,32,45,128]{3,1,2,0:T(8,128)(2,1)}, bf16[2,32,45,128]{3,1,2,0:T(8,128)(2,1)}, u32[]{:S(2)}, u32[]{:S(2)}) collective-permute-start(bf16[2,32,45,128]{3,1,2,0:T(8,128)(2,1)} %param.4), channel_id=1, source_target_pairs={{480,0},{496,16},{0,32},{16,48},{32,64},{48,80},{64,96},{80,112},{... | collective-permute-start | bytes 2211848 | tf_op jit(solution)/shard_map/ppermute | solution.py:13
  18.1 50.5 %collective-permute-start.3 = (bf16[2,32,45,128]{3,1,2,0:T(8,128)(2,1)}, bf16[2,32,45,128]{3,1,2,0:T(8,128)(2,1)}, u32[]{:S(2)}, u32[]{:S(2)}) collective-permute-start(bf16[2,32,45,128]{3,1,2,0:T(8,128)(2,1)} %param.4), channel_id=1, source_target_pairs={{32,0},{48,16},{64,32},{80,48},{96,64},{112,80},{128,96},{144,112}... | collective-permute-start | bytes 2211848 | tf_op jit(solution)/shard_map/ppermute | solution.py:13
  103.4 11.5 %copy-start.2 = (bf16[32,16,3,3]{0,1,3,2:T(8,128)(2,1)S(1)}, bf16[32,16,3,3]{0,1,3,2:T(8,128)(2,1)}, u32[]{:S(2)}) copy-start(bf16[32,16,3,3]{0,1,3,2:T(8,128)(2,1)} %param.6) | copy-start | bytes 27652
  106.4 8.6 %collective-permute-start.4 = (bf16[2,32,4,128]{3,2,0,1:T(4,128)(2,1)S(1)}, bf16[2,32,4,128]{3,2,0,1:T(4,128)(2,1)S(1)}, u32[]{:S(2)}, u32[]{:S(2)}) collective-permute-start(bf16[2,32,4,128]{3,2,0,1:T(4,128)(2,1)S(1)} %get-tuple-element.16), channel_id=1, source_target_pairs={{0,16},{16,32},{32,48},{48,64},{64,80},{80,96},{96,112},{112,128},... | collective-permute-start | bytes 196616 | tf_op jit(solution)/shard_map/ppermute | solution.py:22
  108.3 8.2 %collective-permute-start.5 = (bf16[2,32,4,128]{3,2,0,1:T(4,128)(2,1)S(1)}, bf16[2,32,4,128]{3,2,0,1:T(4,128)(2,1)S(1)}, u32[]{:S(2)}, u32[]{:S(2)}) collective-permute-start(bf16[2,32,4,128]{3,2,0,1:T(4,128)(2,1)S(1)} %get-tuple-element.17), channel_id=1, source_target_pairs={{16,0},{32,16},{48,32},{64,48},{80,64},{96,80},{112,96},{128,112},... | collective-permute-start | bytes 196616 | tf_op jit(solution)/shard_map/ppermute | solution.py:25
  124.3 279.1 %copy-start.1 = (bf16[2,32,45,128]{3,1,2,0:T(8,128)(2,1)S(1)}, bf16[2,32,45,128]{3,1,2,0:T(8,128)(2,1)}, u32[]{:S(2)}) copy-start(bf16[2,32,45,128]{3,1,2,0:T(8,128)(2,1)} %param.4) | copy-start | bytes 2211844
Sparse Core Ops, SparseCore 0:
  128.5 274.8 all-gather.1
where the time goes:
time: 420 us; the launch traced here: 418 us
  waiting for transfers between devices  277 us (66%)
  local copies, waits for them, and re-layouts  81.2 us (19%)
  starting transfers between devices  26.6 us (6%)
  matrix products  14 us (3%)
  between operations  13.6 us (3%)
  other arithmetic  5.55 us (1%)
    all_gather x1, waiting for transfers between devices, per_device(): lax.all_gather(hidden, 'ch', axis=1, tiled=True)  275 us
    gather x3, local copies, waits for them, and re-layouts, per_device(): zonal_taps[:, clipped]  35.9 us
    concatenate x1, local copies, waits for them, and re-layouts, per_device(): jnp.concatenate([sides[2], sides[1], fields, sides[-1], sides[-2]], axis=2)  32.4 us
    ppermute x4, starting transfers between devices, passed_along(): return lax.ppermute(block, axis, route)  18.2 us
  transfers between devices with their start and end apart: 7, of which 2 were waited for; matrix products, arithmetic and copies ran while one was open for 11% of the time, Pallas kernels for 0%

commit v1 on v0

--- a/solution.py
+++ b/solution.py
@@ -72,12 +72,24 @@
     hidden = jax.nn.gelu(
         summed.reshape(ensemble_members, chans, field_width, row_block), approximate=False
     ).astype(jnp.bfloat16)
-    mixed = jnp.einsum(
-        "oi,milr->molr",
-        mix_weight,
-        lax.all_gather(hidden, "ch", axis=1, tiled=True),
+    count = lax.axis_size("ch")
+    rows = ensemble_members * field_width
+    share = -(-rows // count)
+    by_row = hidden.transpose(0, 2, 1, 3).reshape(rows, chans, row_block)
+    by_row = jnp.pad(by_row, ((0, count * share - rows), (0, 0), (0, 0)))
+    gathered = lax.all_to_all(
+        by_row.reshape(count, share, chans, row_block), "ch", 0, 0, tiled=True
+    )
+    mix_full = lax.all_gather(mix_weight, "ch", axis=0, tiled=True)
+    mixed_rows = jnp.einsum(
+        "doci,csir->dsor",
+        mix_full.reshape(count, chans, count, chans),
+        gathered,
         preferred_element_type=jnp.float32,
     ).astype(jnp.bfloat16)
+    returned = lax.all_to_all(mixed_rows, "ch", 0, 0, tiled=True)
+    returned = returned.reshape(count * share, chans, row_block)[:rows]
+    mixed = returned.reshape(ensemble_members, field_width, chans, row_block).transpose(0, 2, 1, 3)
     return (fields.astype(jnp.float32) + mixed.astype(jnp.float32)).astype(jnp.bfloat16)
 
 

time: 420 us -> 229 us (0.55)
  waiting for transfers between devices: 277 us -> 1.59 us
  blocking collectives: 0 us -> 90.2 us
  between operations: 13.6 us -> 0.33 us
  starting transfers between devices: 26.6 us -> 38.3 us
  matrix products: 14 us -> 7.64 us
    all_gather x1 -> x0, waiting for transfers between devices: 275 us -> none  [per_device(): lax.all_gather(hidden, 'ch', axis=1, tiled=True)]
    all_gather x0 -> x1, blocking collectives: none -> 66.1 us  [per_device(): mix_full = lax.all_gather(mix_weight, 'ch', axis=0, tiled=True)]
    all_to_all x0 -> x1, blocking collectives: none -> 24.1 us  [per_device(): returned = lax.all_to_all(mixed_rows, 'ch', 0, 0, tiled=True)]
    all_to_all x0 -> x1, starting transfers between devices: none -> 14.1 us  [per_device(): lax.all_to_all(by_row.reshape(count, share, chans, row_block), 'ch', 0, 0...]
    dot_general x1, matrix products: 7.34 us -> 1.04 us  [per_device(): jnp.einsum('doci,csir->dsor', mix_full.reshape(count, chans, count, chans...]
  transfers between devices with their start and end apart: 7 -> 7, of which waited for: 2 -> 1; matrix products, arithmetic and copies ran while one was open for 11% -> 20% of each run, Pallas kernels for 0% -> 0%
where the time goes in v1:
time: 229 us; the launch traced here: 226 us
  blocking collectives  90.2 us (39%)
  local copies, waits for them, and re-layouts  82.3 us (36%)
  starting transfers between devices  38.3 us (17%)
  matrix products  7.64 us (3%)
  other arithmetic  5.88 us (3%)
    all_gather x1, blocking collectives, per_device(): mix_full = lax.all_gather(mix_weight, 'ch', axis=0, tiled=True)  66.1 us
    gather x3, local copies, waits for them, and re-layouts, per_device(): zonal_taps[:, clipped]  35.9 us
    concatenate x1, local copies, waits for them, and re-layouts, per_device(): jnp.concatenate([sides[2], sides[1], fields, sides[-1], sides[-2]], axis=2)  31.2 us
    all_to_all x1, blocking collectives, per_device(): returned = lax.all_to_all(mixed_rows, 'ch', 0, 0, tiled=True)  24.1 us
    ppermute x4, starting transfers between devices, passed_along(): return lax.ppermute(block, axis, route)  15.8 us
    all_to_all x1, starting transfers between devices, per_device(): lax.all_to_all(by_row.reshape(count, share, chans, row_block), 'ch', 0, 0...  14.1 us
    ppermute x4, local copies, waits for them, and re-layouts, passed_along(): return lax.ppermute(block, axis, route)  8.35 us
    ppermute x1, starting transfers between devices, extended(): lax.ppermute(lax.slice_in_dim(block, 0, width, axis=dim), axis, backward)  6.52 us
  transfers between devices with their start and end apart: 7, of which 1 were waited for; matrix products, arithmetic and copies ran while one was open for 20% of the time, Pallas kernels for 0%

profile of v1, /device:TPU:6, one launch (start us, length us, event | category | flops | bytes accessed | tf_op | source)
XLA Modules:
  0.0 226.2 jit_solution(9865625845167970870)
XLA Ops:
  0.0 4.4 %collective-permute-start = (bf16[2,32,45,128]{3,1,2,0:T(8,128)(2,1)}, bf16[2,32,45,128]{3,1,2,0:T(8,128)(2,1)}, u32[]{:S(2)}, u32[]{:S(2)}) collective-permute-start(bf16[2,32,45,128]{3,1,2,0:T(8,128)(2,1)} %param.4), channel_id=1, source_target_pairs={{480,0},{496,16},{0,32},{16,48},{32,64},{48,80},{64,96},{80,112},{... | collective-permute-start | bytes 2211848 | tf_op jit(solution)/shard_map/ppermute | solution.py:13
  4.4 1.9 collective-permute-start.1
  6.3 6.3 %collective-permute-start.2 = (bf16[2,32,45,128]{3,1,2,0:T(8,128)(2,1)}, bf16[2,32,45,128]{3,1,2,0:T(8,128)(2,1)}, u32[]{:S(2)}, u32[]{:S(2)}) collective-permute-start(bf16[2,32,45,128]{3,1,2,0:T(8,128)(2,1)} %param.4), channel_id=1, source_target_pairs={{16,0},{32,16},{48,32},{64,48},{80,64},{96,80},{112,96},{128,112},... | collective-permute-start | bytes 2211848 | tf_op jit(solution)/shard_map/ppermute | solution.py:13
  12.7 3.1 %collective-permute-start.3 = (bf16[2,32,45,128]{3,1,2,0:T(8,128)(2,1)}, bf16[2,32,45,128]{3,1,2,0:T(8,128)(2,1)}, u32[]{:S(2)}, u32[]{:S(2)}) collective-permute-start(bf16[2,32,45,128]{3,1,2,0:T(8,128)(2,1)} %param.4), channel_id=1, source_target_pairs={{32,0},{48,16},{64,32},{80,48},{96,64},{112,80},{128,96},{144,112}... | collective-permute-start | bytes 2211848 | tf_op jit(solution)/shard_map/ppermute | solution.py:13
  15.8 1.4 copy.49
  17.6 30.4 %gather_fusion = bf16[10125,32]{1,0:T(8,128)(2,1)S(1)} fusion(bf16[32,181]{0,1:T(8,128)(2,1)S(1)} %copy.45, s32[10240]{0:T(1024)S(1)} %pad_clamp_fusion), kind=kCustom, calls=%fused_computation | custom fusion | bytes 1336500 | tf_op jit(solution)/shard_map/gather | solution.py:39
  48.1 2.8 %copy.46 = bf16[10125,32]{0,1:T(8,128)(2,1)} copy(bf16[10125,32]{1,0:T(8,128)(2,1)S(1)} %gather_fusion) | data formatting | bytes 1296000 | tf_op jit(solution)/shard_map/gather | solution.py:39
  50.9 2.7 %reshape.81 = bf16[225,45,32]{1,0,2:T(8,128)(2,1)S(1)} reshape(bf16[10125,32]{0,1:T(8,128)(2,1)} %copy.46) | data formatting | bytes 1296000 | tf_op jit(solution)/shard_map/gather | solution.py:39
  53.6 1.4 copy.47
  55.1 2.3 %copy.48 = bf16[2,32,45,128]{3,2,0,1:T(8,128)(2,1)} copy(bf16[2,32,45,128]{3,1,2,0:T(8,128)(2,1)} %collective-permute-done.1) | data formatting | bytes 1474560 | tf_op jit(solution)/shard_map/ppermute | solution.py:13
  57.4 2.3 %copy.50 = bf16[2,32,45,128]{3,2,0,1:T(8,128)(2,1)} copy(bf16[2,32,45,128]{3,1,2,0:T(8,128)(2,1)} %collective-permute-done.2) | data formatting | bytes 1474560 | tf_op jit(solution)/shard_map/ppermute | solution.py:13
  59.7 2.3 %copy.51 = bf16[2,32,45,128]{3,2,0,1:T(8,128)(2,1)} copy(bf16[2,32,45,128]{3,1,2,0:T(8,128)(2,1)} %collective-permute-done.3) | data formatting | bytes 1474560 | tf_op jit(solution)/shard_map/ppermute | solution.py:13
  62.0 31.2 %concatenate.6 = bf16[2,32,225,128]{3,2,0,1:T(8,128)(2,1)} concatenate(bf16[2,32,45,128]{3,2,0,1:T(8,128)(2,1)S(1)} %copy.47, bf16[2,32,45,128]{3,2,0,1:T(8,128)(2,1)} %copy.48, bf16[2,32,45,128]{3,2,0,1:T(8,128)(2,1)S(1)} %copy.49, bf16[2,32,45,128]{3,2,0,1:T(8,128)(2,1)} %copy.50, bf16[2,32,45,128]{3,2,0,1:T(8,128)(2,1)} %copy.51), dimensions={2} | concatenate | bytes 7372800 | tf_op jit(solution)/shard_map/concatenate | solution.py:35
  93.2 2.9 %fusion.37 = bf16[2,32,45,128]{3,2,0,1:T(8,128)(2,1)S(1)} fusion(bf16[2,32,225,128]{3,2,0,1:T(8,128)(2,1)} %concatenate.6, bf16[225,45,32]{1,0,2:T(8,128)(2,1)S(1)} %reshape.81, pred[225,45]{1,0:T(8,128)(4,1)S(1)} %fusion.64), kind=kOutput, calls=%fused_computation.46 | convolution fusion | flops 166580640 | bytes 5081805 | tf_op jit(solution)/shard_map/mcjr,cjl->mclr/dot_general | solution.py:40
  96.2 1.9 collective-permute-start.4
  98.1 6.5 %collective-permute-start.5 = (bf16[2,32,4,128]{3,2,0,1:T(4,128)(2,1)S(1)}, bf16[2,32,4,128]{3,2,0,1:T(4,128)(2,1)S(1)}, u32[]{:S(2)}, u32[]{:S(2)}) collective-permute-start(bf16[2,32,4,128]{3,2,0,1:T(4,128)(2,1)S(1)} %get-tuple-element.17), channel_id=1, source_target_pairs={{16,0},{32,16},{48,32},{64,48},{80,64},{96,80},{112,96},{128,112},... | collective-permute-start | bytes 196616 | tf_op jit(solution)/shard_map/ppermute | solution.py:25
  104.7 1.6 collective-permute-done.5
  106.3 1.4 fusion.12
  107.8 2.2 fusion.66
  110.0 0.4 fusion.46
  110.7 0.4 fusion.50
  111.8 0.4 fusion.56
  112.5 0.4 fusion.60
  112.9 0.8 multiply_bitcast_fusion.1
  114.1 3.3 %fusion.17 = bf16[2,32,45,128]{3,1,2,0:T(8,128)(2,1)S(1)} fusion(f32[2,2,16,45,128]{4,2,1,3,0:T(8,128)S(1)} %copy.64, f32[2,2,16,45,128]{4,2,1,3,0:T(8,128)S(1)} %copy.63), kind=kLoop, calls=%fused_computation.20 | loop fusion | flops 22855680 | bytes 3686400 | tf_op jit(solution)/shard_map/convert_element_type | solution.py:74
  117.5 1.0 pad.9
  118.4 14.1 %all-to-all-start = ((bf16[16,6,32,128]{3,2,1,0:T(8,128)(2,1)}), bf16[16,6,32,128]{3,2,1,0:T(8,128)(2,1)S(1)}, u32[]{:S(2)}, u32[]{:S(2)}) async-start(bf16[16,6,32,128]{3,2,1,0:T(8,128)(2,1)} %bitcast.38), calls=%async_computation | async-start | bytes 1572864 | tf_op jit(solution)/shard_map/all_to_all | solution.py:80
  132.6 66.1 %all_gather.3 = bf16[512,512]{1,0:T(8,128)(2,1)S(1)} all-gather(bf16[32,512]{1,0:T(8,128)(2,1)S(1)} %copy-done.2), channel_id=1, replica_groups=mesh['lon'=32,'ch'=16] {'ch'}, dimensions={0}, use_global_device_ids=true | all-gather | bytes 557056 | tf_op jit(solution)/shard_map/all_gather | solution.py:83
  198.7 1.2 reshape.74
  199.9 1.0 fusion.40
  201.0 24.1 %all_to_all.10 = bf16[16,6,32,128]{3,2,1,0:T(8,128)(2,1)S(1)} all-to-all(bf16[16,6,32,128]{3,2,1,0:T(8,128)(2,1)S(1)} %copy.67), channel_id=1, replica_groups=mesh['lon'=32,'ch'=16] {'ch'}, dimensions={0} | all-to-all | bytes 1572864 | tf_op jit(solution)/shard_map/all_to_all | solution.py:90
  225.2 1.1 fusion.19
  (29 shorter events, 2.6 us)
Async XLA Ops:
  0.0 17.5 %copy-start.3 = (bf16[32,181]{1,0:T(8,128)(2,1)S(1)}, bf16[32,181]{1,0:T(8,128)(2,1)}, u32[]{:S(2)}) copy-start(bf16[32,181]{1,0:T(8,128)(2,1)} %param.5) | copy-start | bytes 34756
  0.0 53.6 %collective-permute-start = (bf16[2,32,45,128]{3,1,2,0:T(8,128)(2,1)}, bf16[2,32,45,128]{3,1,2,0:T(8,128)(2,1)}, u32[]{:S(2)}, u32[]{:S(2)}) collective-permute-start(bf16[2,32,45,128]{3,1,2,0:T(8,128)(2,1)} %param.4), channel_id=1, source_target_pairs={{480,0},{496,16},{0,32},{16,48},{32,64},{48,80},{64,96},{80,112},{... | collective-permute-start | bytes 2211848 | tf_op jit(solution)/shard_map/ppermute | solution.py:13
  4.4 50.6 %collective-permute-start.1 = (bf16[2,32,45,128]{3,1,2,0:T(8,128)(2,1)}, bf16[2,32,45,128]{3,1,2,0:T(8,128)(2,1)}, u32[]{:S(2)}, u32[]{:S(2)}) collective-permute-start(bf16[2,32,45,128]{3,1,2,0:T(8,128)(2,1)} %param.4), channel_id=1, source_target_pairs={{496,0},{0,16},{16,32},{32,48},{48,64},{64,80},{80,96},{96,112},{1... | collective-permute-start | bytes 2211848 | tf_op jit(solution)/shard_map/ppermute | solution.py:13
  6.3 51.0 %collective-permute-start.2 = (bf16[2,32,45,128]{3,1,2,0:T(8,128)(2,1)}, bf16[2,32,45,128]{3,1,2,0:T(8,128)(2,1)}, u32[]{:S(2)}, u32[]{:S(2)}) collective-permute-start(bf16[2,32,45,128]{3,1,2,0:T(8,128)(2,1)} %param.4), channel_id=1, source_target_pairs={{16,0},{32,16},{48,32},{64,48},{80,64},{96,80},{112,96},{128,112},... | collective-permute-start | bytes 2211848 | tf_op jit(solution)/shard_map/ppermute | solution.py:13
  12.7 47.0 %collective-permute-start.3 = (bf16[2,32,45,128]{3,1,2,0:T(8,128)(2,1)}, bf16[2,32,45,128]{3,1,2,0:T(8,128)(2,1)}, u32[]{:S(2)}, u32[]{:S(2)}) collective-permute-start(bf16[2,32,45,128]{3,1,2,0:T(8,128)(2,1)} %param.4), channel_id=1, source_target_pairs={{32,0},{48,16},{64,32},{80,48},{96,64},{112,80},{128,96},{144,112}... | collective-permute-start | bytes 2211848 | tf_op jit(solution)/shard_map/ppermute | solution.py:13
  93.2 11.5 %copy-start.1 = (bf16[32,16,3,3]{0,1,3,2:T(8,128)(2,1)S(1)}, bf16[32,16,3,3]{0,1,3,2:T(8,128)(2,1)}, u32[]{:S(2)}) copy-start(bf16[32,16,3,3]{0,1,3,2:T(8,128)(2,1)} %param.6) | copy-start | bytes 27652
  96.2 8.6 %collective-permute-start.4 = (bf16[2,32,4,128]{3,2,0,1:T(4,128)(2,1)S(1)}, bf16[2,32,4,128]{3,2,0,1:T(4,128)(2,1)S(1)}, u32[]{:S(2)}, u32[]{:S(2)}) collective-permute-start(bf16[2,32,4,128]{3,2,0,1:T(4,128)(2,1)S(1)} %get-tuple-element.16), channel_id=1, source_target_pairs={{0,16},{16,32},{32,48},{48,64},{64,80},{80,96},{96,112},{112,128},... | collective-permute-start | bytes 196616 | tf_op jit(solution)/shard_map/ppermute | solution.py:22
  98.1 8.2 %collective-permute-start.5 = (bf16[2,32,4,128]{3,2,0,1:T(4,128)(2,1)S(1)}, bf16[2,32,4,128]{3,2,0,1:T(4,128)(2,1)S(1)}, u32[]{:S(2)}, u32[]{:S(2)}) collective-permute-start(bf16[2,32,4,128]{3,2,0,1:T(4,128)(2,1)S(1)} %get-tuple-element.17), channel_id=1, source_target_pairs={{16,0},{32,16},{48,32},{64,48},{80,64},{96,80},{112,96},{128,112},... | collective-permute-start | bytes 196616 | tf_op jit(solution)/shard_map/ppermute | solution.py:25
  117.4 15.1 %copy-start.2 = (bf16[32,512]{1,0:T(8,128)(2,1)S(1)}, bf16[32,512]{1,0:T(8,128)(2,1)}, u32[]{:S(2)}) copy-start(bf16[32,512]{1,0:T(8,128)(2,1)} %param.7) | copy-start | bytes 98308
  118.4 81.5 %all-to-all-start = ((bf16[16,6,32,128]{3,2,1,0:T(8,128)(2,1)}), bf16[16,6,32,128]{3,2,1,0:T(8,128)(2,1)S(1)}, u32[]{:S(2)}, u32[]{:S(2)}) async-start(bf16[16,6,32,128]{3,2,1,0:T(8,128)(2,1)} %bitcast.38), calls=%async_computation | async-start | bytes 1572864 | tf_op jit(solution)/shard_map/all_to_all | solution.py:80
  201.0 24.1 %copy-start = (bf16[2,32,45,128]{3,1,2,0:T(8,128)(2,1)S(1)}, bf16[2,32,45,128]{3,1,2,0:T(8,128)(2,1)}, u32[]{:S(2)}) copy-start(bf16[2,32,45,128]{3,1,2,0:T(8,128)(2,1)} %param.4) | copy-start | bytes 2211844

commit v2 on v0

v2 whole, which is shorter than its diff:
```python
import jax
import jax.numpy as jnp
from jax import lax
from jax.experimental import pallas as pl
from jax.experimental.pallas import tpu as pltpu
from jax.sharding import Mesh, PartitionSpec as P

F32, BF16 = jnp.float32, jnp.bfloat16
MEMBERS, CHANS, WIDTH, LAT = 2, 32, 45, 128
SLOT = 48
GROUP = 16
TALL = 56
BLOCKS = 8
VMEM = pltpu.CompilerParams(vmem_limit_bytes=40 * 1024 * 1024)
CHIPS = (("x", 4), ("zl", 4), ("core", 2), ("zh", 2), ("y", 8))


def lat_shuffle(back):
    rows = lax.broadcasted_iota(jnp.int32, (256, 256), 1 if back else 0)
    cols = lax.broadcasted_iota(jnp.int32, (256, 256), 0 if back else 1)
    chan, lane = (cols % 128) // 64, cols % 64
    source = chan * 128 + 4 * (lane // 2) + 2 * (cols // 128) + lane % 2
    return jnp.where(rows == source, 1.0, 0.0).astype(BF16)


def split_kernel(fields_ref, out_ref, wide):
    shuffle = lat_shuffle(False)
    wide[...] = fields_ref[...].astype(F32).reshape(MEMBERS, WIDTH * CHANS, 128)
    for m in range(MEMBERS):
        for g in range(2):
            for c in range(8):
                sides = [
                    wide[m, pl.ds(g * GROUP + part * 8 + c, WIDTH, stride=CHANS), :].astype(BF16)
                    for part in range(2)
                ]
                both = jnp.concatenate(sides, axis=1)
                moved = jnp.dot(both, shuffle, preferred_element_type=F32).astype(BF16)
                for s in range(2):
                    out_ref[m, s, g, c, 32:48] = jnp.zeros((16, 128), BF16)
                    out_ref[m, s, g, c, 0:WIDTH] = moved[:, s * 128 : s * 128 + 128]


def toeplitz_kernel(taps_ref, out_ref):
    lane = lax.broadcasted_iota(jnp.int32, (TALL, 256), 1)
    for c in range(GROUP):
        row = jnp.broadcast_to(taps_ref[c : c + 1, :], (TALL, 256))
        base = pltpu.roll(row, 0, 1, stride=1, stride_axis=0)
        full = pltpu.roll(base, 252, 1)
        for k in range(1, 5):
            full = jnp.where(lane >= SLOT * k, pltpu.roll(base, (3 * k - 4) % 256, 1), full)
        full = jnp.where(lane >= 240, pltpu.roll(base, 11, 1), full)
        full = jnp.where(lane >= 248, pltpu.roll(base, 249, 1), full)
        out_ref[c] = full.astype(BF16)


def turned(v):
    return jnp.concatenate([v[:, 64:], v[:, :64]], axis=1)


def rim_kernel(run_ref, unused_ref, low_ref, high_ref):
    low_ref[:, 0:16] = run_ref[5, :, 32:48]
    low_ref[:, 16:64] = run_ref[6]
    low_ref[:, 64:112] = run_ref[7]
    high_ref[:, 0:48] = run_ref[0]
    high_ref[:, 48:96] = run_ref[1]
    high_ref[:, 96:112] = run_ref[2, :, 0:16]


def conv_kernel(unused_ref, low_ref, mid_ref, high_ref, toep_ref, weight_ref, out_ref, zonal, shifted):
    lane = lax.broadcasted_iota(jnp.int32, (SLOT, 128), 1)
    first_half = lane < 64
    tile_row = lax.broadcasted_iota(jnp.int32, (16, 128), 0)

    def block(b, c):
        if 0 <= b < BLOCKS:
            return mid_ref[b, c]
        if b < 0:
            return low_ref[c, 16 + SLOT * (b + 2) : 16 + SLOT * (b + 3)]
        return high_ref[c, SLOT * (b - BLOCKS) : SLOT * (b - BLOCKS + 1)]

    def one_pair(c):
        blocks = {b: block(b, c) for b in range(-2, BLOCKS + 2)}
        tails = {b: blocks[b][32:48] if b >= -2 else low_ref[c, 0:16] for b in range(-3, 5)}
        heads = {
            b: blocks[b][0:16] if b < BLOCKS + 2 else high_ref[c, 2 * SLOT : 2 * SLOT + 16]
            for b in range(3, BLOCKS + 3)
        }
        blocks_turned = {b: turned(v) for b, v in blocks.items()}
        tails_turned = {b: turned(v) for b, v in tails.items()}
        heads_turned = {b: turned(v) for b, v in heads.items()}
        for part in range(2):

            def paired(plain, other, b):
                low, high = (plain, other) if part == 0 else (other, plain)
                return jnp.where(first_half[: low[b].shape[0]], low[b], high[b + 4])

            wide = {b: paired(blocks, blocks_turned, b) for b in range(-2, 6)}
            taps = toep_ref[part * 8 + c]
            for b in range(4):
                rim = jnp.where(
                    tile_row >= 8,
                    paired(tails, tails_turned, b - 3),
                    paired(heads, heads_turned, b + 3),
                )
                window = jnp.concatenate([wide[b + k] for k in range(-2, 3)] + [rim], axis=0)
                result = jnp.dot(taps, window, preferred_element_type=F32)
                zonal[pl.ds(b * TALL * GROUP + part * 8 + c, TALL, stride=GROUP), :] = result

    for c in range(8):
        one_pair(c)

    place = lax.broadcasted_iota(jnp.int32, (TALL * GROUP, 128), 1) % 64
    for b in range(4):
        z = zonal[b * TALL * GROUP : (b + 1) * TALL * GROUP, :]
        south = jnp.where(place < 2, 0.0, pltpu.roll(z, 2, 1))
        north = jnp.where(place >= 62, 0.0, pltpu.roll(z, 126, 1))
        for a, v in enumerate((south, z, north)):
            shifted[b, a] = v.astype(BF16).reshape(TALL, GROUP, 128)

    weight = weight_ref[...]

    def three_columns(n, carry):
        for half in range(2):
            for i in range(3):
                col = n * 3 + i
                sides = []
                for top in range(2):
                    tiles = [
                        shifted[half + 2 * top, a, col + 4 * b] for b in range(3) for a in range(3)
                    ]
                    sides.append(jnp.concatenate(tiles, axis=0))
                x = jnp.dot(weight, jnp.concatenate(sides, axis=1), preferred_element_type=F32)
                x = 0.5 * x * (1.0 + lax.erf(x * 0.7071067811865476))
                x = x.astype(BF16)
                for top in range(2):
                    out_ref[half * 16 + n, top * 3 + i] = x[:, top * 128 : top * 128 + 128]
        return carry

    lax.fori_loop(0, 15, three_columns, 0)
    for half in range(2):
        for i in range(6):
            out_ref[half * 16 + 15, i] = jnp.zeros((GROUP, 128), BF16)


def mix_kernel(owner_ref, weight_ref, hidden_ref, out_ref):
    first_half = lax.broadcasted_iota(jnp.int32, (GROUP, 128), 1) < 64
    weight = weight_ref[...].reshape(512, 512)
    for i in range(3):
        cols = [hidden_ref[:, top * 3 + i].reshape(512, 128) for top in range(2)]
        y = jnp.dot(weight, jnp.concatenate(cols, axis=1), preferred_element_type=F32)
        y = y.astype(BF16)
        for ch in range(16):
            owner = owner_ref[ch]
            for top in range(2):
                a = y[ch * 32 : ch * 32 + 16, top * 128 : top * 128 + 128]
                b = y[ch * 32 + 16 : ch * 32 + 32, top * 128 : top * 128 + 128]
                out_ref[top, owner, i] = jnp.where(first_half, a, turned(b))
                out_ref[2 + top, owner, i] = jnp.where(first_half, turned(a), b)


def join_kernel(mixed_ref, fields_ref, out_ref):
    shuffle = lat_shuffle(True)
    for m in range(MEMBERS):
        both = jnp.concatenate(
            [mixed_ref[m, s, 0:WIDTH].reshape(WIDTH * GROUP, 128) for s in range(2)], axis=1
        )
        y = jnp.dot(both, shuffle, preferred_element_type=F32).reshape(WIDTH, GROUP, 256)
        for part in range(2):
            rows = slice(part * GROUP, part * GROUP + GROUP)
            total = fields_ref[m, :, rows].astype(F32) + y[:, :, part * 128 : part * 128 + 128]
            out_ref[m, :, rows] = total.astype(BF16)


def kernel_call(body, shape, scratch=(), cost=(0, 0), **specs):
    return pl.pallas_call(
        body,
        **specs,
        out_shape=shape if isinstance(shape, list) else jax.ShapeDtypeStruct(shape, BF16),
        scratch_shapes=list(scratch),
        compiler_params=VMEM,
        cost_estimate=pl.CostEstimate(flops=cost[0], bytes_accessed=cost[1], transcendentals=0),
    )


def with_behind(blocks, axis, *steps):
    count = lax.axis_size(axis)
    parts = [blocks]
    for step in steps:
        parts.append(lax.ppermute(blocks, axis, [(i, (i + step) % count) for i in range(count)]))
    return jnp.concatenate(parts, axis=0)


def block_owners():
    i = jnp.arange(16)
    zh = (lax.axis_index("zh") + i // 8) % 2
    y = (lax.axis_index("y") - 2 * (i % 4) - i // 4 % 2) % 8
    return (zh * 8 + y).astype(jnp.int32)


def per_device(fields, zonal_taps, conv_weight, mix_weight):
    core = lax.axis_index("core")
    vmem = pl.BlockSpec(memory_space=pltpu.VMEM)
    loose = pl.BlockSpec(memory_space=pl.ANY)
    by_group = mix_weight.reshape(CHANS, 16, 2, GROUP).transpose(0, 2, 1, 3).reshape(CHANS, 512)
    few = with_behind(with_behind(by_group[None], "y", 2, 4, 6), "y", 1)
    mix_full = with_behind(few, "zh", 1)

    columns = fields.transpose(0, 2, 1, 3)
    units = kernel_call(
        split_kernel,
        (2, 2, 2, 8, SLOT, 128),
        scratch=(pltpu.VMEM((MEMBERS, WIDTH * CHANS, 128), F32),),
        cost=(2 * 10**8, 3 * 10**6),
    )(columns)
    run = lax.all_to_all(
        units.reshape(BLOCKS, 8, SLOT, 128), ("zl", "core"), 0, 0, tiled=True
    )
    taps = lax.dynamic_slice_in_dim(zonal_taps, core * GROUP, GROUP, 0).astype(F32)
    taps = jnp.pad(taps, ((0, 0), (0, 256 - taps.shape[1])))
    toeplitz = kernel_call(toeplitz_kernel, (GROUP, TALL, 256), cost=(10**7, 10**6))(taps)
    weight = lax.dynamic_slice_in_dim(conv_weight, core * GROUP, GROUP, 0)
    weight = weight.transpose(0, 3, 2, 1).reshape(GROUP, 9 * GROUP)

    count = lax.axis_size("x")
    east = [(i, (i + 1) % count) for i in range(count)]
    west = [(b, a) for a, b in east]
    rim = jax.ShapeDtypeStruct((8, 112, 128), BF16)
    low, high = kernel_call(rim_kernel, [rim, rim], in_specs=[vmem, loose], cost=(0, 10**6))(run, few)
    low = lax.ppermute(low, "x", east)
    high = lax.ppermute(high, "x", west)

    hidden = kernel_call(
        conv_kernel,
        (32, 6, GROUP, 128),
        scratch=(
            pltpu.VMEM((4 * TALL * GROUP, 128), F32),
            pltpu.VMEM((4, 3, TALL, GROUP, 128), BF16),
        ),
        cost=(10**9, 3 * 10**6),
        in_specs=[loose] + [vmem] * 5,
    )(mix_full, low, run, high, toeplitz, weight)
    gathered = lax.all_to_all(hidden, ("core", "zh", "y"), 0, 0, tiled=True)
    mixed = kernel_call(
        mix_kernel,
        (4, 16, 3, GROUP, 128),
        cost=(4 * 10**8, 2 * 10**6),
        in_specs=[pl.BlockSpec(memory_space=pltpu.SMEM), vmem, vmem],
    )(block_owners(), mix_full, gathered)
    back = lax.all_to_all(mixed.reshape(64, 3, GROUP, 128), ("zl", "zh", "y"), 0, 0, tiled=True)
    updated = kernel_call(join_kernel, columns.shape, cost=(2 * 10**8, 3 * 10**6))(
        back.reshape(MEMBERS, 2, SLOT, GROUP, 128), columns
    )
    return updated.transpose(0, 2, 1, 3)


def solution(mesh):
    names, sizes = zip(*CHIPS)
    chips = Mesh(mesh.devices.reshape(sizes), names)
    lon, ch = ("x", "zl", "core"), ("zh", "y")
    return jax.shard_map(
        per_device,
        mesh=chips,
        in_specs=(P(None, ch, lon, None), P(ch, None), P(ch, None, None, None), P(ch, None)),
        out_specs=P(None, ch, lon, None),
        check_vma=False,
    )
```

time: 420 us -> 131 us (0.31)
  waiting for transfers between devices: 277 us -> 36.9 us
  local copies, waits for them, and re-layouts: 81.2 us -> 2.32 us
  blocking collectives: 0 us -> 30 us
  starting transfers between devices: 26.6 us -> 48.1 us
  matrix products: 14 us -> 0 us
  between operations: 13.6 us -> 0.23 us
  Pallas kernels: 0 us -> 12 us
  other arithmetic: 5.55 us -> 0.04 us
    all_gather x1 -> x0, waiting for transfers between devices: 275 us -> none  [per_device(): lax.all_gather(hidden, 'ch', axis=1, tiled=True)]
    gather x3 -> x0, local copies, waits for them, and re-layouts: 35.9 us -> none  [per_device(): zonal_taps[:, clipped]]
    concatenate x1 -> x2, local copies, waits for them, and re-layouts: 32.4 us -> 0.04 us  [with_behind(): return jnp.concatenate(parts, axis=0)]
    all_to_all x0 -> x1, blocking collectives: none -> 30 us  [per_device(): lax.all_to_all(mixed.reshape(64, 3, GROUP, 128), ('zl', 'zh', 'y'), 0, 0,...]
    all_to_all x0 -> x2, waiting for transfers between devices: none -> 25.6 us  [the longest x1 25.6 us: per_device(): gathered = lax.all_to_all(hidden, ('core', 'zh', 'y'), 0, 0, tiled=True)]
    all_to_all x0 -> x2, starting transfers between devices: none -> 15.8 us  [the longest x1 8.45 us: per_device(): gathered = lax.all_to_all(hidden, ('core', 'zh', 'y'), 0, 0, tiled=True)]
    dot_general x11 -> x0, matrix products: 14 us -> none  [the longest x1 7.34 us: per_device(): jnp.einsum('oi,milr->molr', mix_weight, lax.all_gather(hidden, 'ch', axis...]
    pallas_call x0 -> x6, Pallas kernels: none -> 12 us  [the longest x1 5.57 us: per_device(): kernel_call(conv_kernel, (32, 6, GROUP, 128), scratch=(pltpu.VMEM((4 * TA...]
  transfers between devices with their start and end apart: 7 -> 9, of which waited for: 2 -> 6; matrix products, arithmetic and copies ran while one was open for 11% -> 0% of each run, Pallas kernels for 0% -> 2%
where the time goes in v2:
time: 131 us; the launch traced here: 130 us
  starting transfers between devices  48.1 us (37%)
  waiting for transfers between devices  36.9 us (28%)
  blocking collectives  30 us (23%)
  Pallas kernels  12 us (9%)
  local copies, waits for them, and re-layouts  2.32 us (2%)
    all_to_all x1, blocking collectives, per_device(): lax.all_to_all(mixed.reshape(64, 3, GROUP, 128), ('zl', 'zh', 'y'), 0, 0,...  30 us
    ppermute x5, starting transfers between devices, with_behind(): lax.ppermute(blocks, axis, [(i, (i + step) % count) for i in range(count)])  26.4 us
    all_to_all x1, waiting for transfers between devices, per_device(): gathered = lax.all_to_all(hidden, ('core', 'zh', 'y'), 0, 0, tiled=True)  25.6 us
    all_to_all x1, starting transfers between devices, per_device(): gathered = lax.all_to_all(hidden, ('core', 'zh', 'y'), 0, 0, tiled=True)  8.45 us
    ppermute x5, waiting for transfers between devices, with_behind(): lax.ppermute(blocks, axis, [(i, (i + step) % count) for i in range(count)])  8.25 us
    all_to_all x1, starting transfers between devices, per_device(): lax.all_to_all(units.reshape(BLOCKS, 8, SLOT, 128), ('zl', 'core'), 0, 0,...  7.4 us
    pallas_call x1, Pallas kernels, per_device(): kernel_call(conv_kernel, (32, 6, GROUP, 128), scratch=(pltpu.VMEM((4 * TA...  5.57 us
    ppermute x1, starting transfers between devices, per_device(): high = lax.ppermute(high, 'x', west)  3.46 us
  transfers between devices with their start and end apart: 9, of which 6 were waited for; matrix products, arithmetic and copies ran while one was open for 0% of the time, Pallas kernels for 2%

profile of v2, /device:TPU:6, one launch (start us, length us, event | category | flops | bytes accessed | tf_op | source)
XLA Modules:
  0.0 129.6 jit_solution(14787117642233893444)
XLA Ops:
  0.0 1.1 copy-done.1
  1.1 2.0 %shard_map.46 = bf16[2,2,2,8,48,128]{5,4,3,2,1,0:T(8,128)(2,1)} custom-call(bf16[2,45,32,128]{3,2,1,0:T(8,128)(2,1)S(1)} %bitcast.13), custom_call_target="tpu_custom_call" | custom-call | flops 200000000 | bytes 3000000 | tf_op jit(solution)/shard_map/pallas_call | solution.py:209
  3.1 7.4 %all-to-all-start = ((bf16[8,8,48,128]{3,2,1,0:T(8,128)(2,1)}), bf16[8,8,48,128]{3,2,1,0:T(8,128)(2,1)S(1)}, u32[]{:S(2)}, u32[]{:S(2)}) async-start(bf16[8,8,48,128]{3,2,1,0:T(8,128)(2,1)} %bitcast.4), calls=%async_computation | async-start | bytes 1572864 | tf_op jit(solution)/shard_map/all_to_all | solution.py:215
  10.5 0.1 copy.7
  10.7 0.1 copy.14
  10.7 6.2 %collective-permute-start.2 = (bf16[1,32,512]{2,1,0:T(8,128)(2,1)S(1)}, bf16[1,32,512]{2,1,0:T(8,128)(2,1)S(1)}, u32[]{:S(2)}, u32[]{:S(2)}) collective-permute-start(bf16[1,32,512]{2,1,0:T(8,128)(2,1)S(1)} %copy.14), channel_id=1, source_target_pairs={{0,6},{1,7},{2,0},{3,1},{4,2},{5,3},{6,4},{7,5},{8,14},{9,15},{10,... | collective-permute-start | bytes 98312 | tf_op jit(solution)/shard_map/ppermute | solution.py:189
  16.9 3.8 %collective-permute-start.1 = (bf16[1,32,512]{2,1,0:T(8,128)(2,1)S(1)}, bf16[1,32,512]{2,1,0:T(8,128)(2,1)S(1)}, u32[]{:S(2)}, u32[]{:S(2)}) collective-permute-start(bf16[1,32,512]{2,1,0:T(8,128)(2,1)S(1)} %copy.14), channel_id=1, source_target_pairs={{0,4},{1,5},{2,6},{3,7},{4,0},{5,1},{6,2},{7,3},{8,12},{9,13},{10,... | collective-permute-start | bytes 98312 | tf_op jit(solution)/shard_map/ppermute | solution.py:189
  20.7 4.5 %collective-permute-start = (bf16[1,32,512]{2,1,0:T(8,128)(2,1)S(1)}, bf16[1,32,512]{2,1,0:T(8,128)(2,1)S(1)}, u32[]{:S(2)}, u32[]{:S(2)}) collective-permute-start(bf16[1,32,512]{2,1,0:T(8,128)(2,1)S(1)} %copy.14), channel_id=1, source_target_pairs={{0,2},{1,3},{2,4},{3,5},{4,6},{5,7},{6,0},{7,1},{8,10},{9,11},{10,... | collective-permute-start | bytes 98312 | tf_op jit(solution)/shard_map/ppermute | solution.py:189
  25.3 0.0 collective-permute-done.2
  25.3 1.4 %collective-permute-done.1 = bf16[1,32,512]{2,1,0:T(8,128)(2,1)S(1)} collective-permute-done((bf16[1,32,512]{2,1,0:T(8,128)(2,1)S(1)}, bf16[1,32,512]{2,1,0:T(8,128)(2,1)S(1)}, u32[]{:S(2)}, u32[]{:S(2)}) %collective-permute-start.1) | collective-permute-done | bytes 32800 | tf_op jit(solution)/shard_map/ppermute | solution.py:189
  26.6 2.0 %collective-permute-done = bf16[1,32,512]{2,1,0:T(8,128)(2,1)S(1)} collective-permute-done((bf16[1,32,512]{2,1,0:T(8,128)(2,1)S(1)}, bf16[1,32,512]{2,1,0:T(8,128)(2,1)S(1)}, u32[]{:S(2)}, u32[]{:S(2)}) %collective-permute-start) | collective-permute-done | bytes 32800 | tf_op jit(solution)/shard_map/ppermute | solution.py:189
  28.7 3.7 %collective-permute-start.3 = (bf16[4,32,512]{2,1,0:T(8,128)(2,1)S(1)}, bf16[4,32,512]{2,1,0:T(8,128)(2,1)S(1)}, u32[]{:S(2)}, u32[]{:S(2)}) collective-permute-start(bf16[4,32,512]{2,1,0:T(8,128)(2,1)S(1)} %pad_maximum_fusion), channel_id=1, source_target_pairs={{0,1},{1,2},{2,3},{3,4},{4,5},{5,6},{6,7},{7,0},{8,9},{9,10},{10,1... | collective-permute-start | bytes 393224 | tf_op jit(solution)/shard_map/ppermute | solution.py:189
  32.4 4.3 %collective-permute-done.3 = bf16[4,32,512]{2,1,0:T(8,128)(2,1)S(1)} collective-permute-done((bf16[4,32,512]{2,1,0:T(8,128)(2,1)S(1)}, bf16[4,32,512]{2,1,0:T(8,128)(2,1)S(1)}, u32[]{:S(2)}, u32[]{:S(2)}) %collective-permute-start.3) | collective-permute-done | bytes 131104 | tf_op jit(solution)/shard_map/ppermute | solution.py:189
  36.8 8.2 %collective-permute-start.4 = (bf16[8,32,512]{2,1,0:T(8,128)(2,1)S(1)}, bf16[8,32,512]{2,1,0:T(8,128)(2,1)S(1)}, u32[]{:S(2)}, u32[]{:S(2)}) collective-permute-start(bf16[8,32,512]{2,1,0:T(8,128)(2,1)S(1)} %get-tuple-element.9.unused_ref), channel_id=1, source_target_pairs={{0,8},{8,0},{1,9},{9,1},{2,10},{10,2},{3,11},{11,3},{4,12},{12,4},... | collective-permute-start | bytes 786440 | tf_op jit(solution)/shard_map/ppermute | solution.py:189
  45.0 0.1 dynamic-slice_bitcast_fusion
  45.1 0.1 copy.15
  45.2 0.0 copy-start.4
  45.2 0.1 reshape.17.weight_ref
  45.3 0.6 copy-done.4
  46.0 2.4 %collective-permute-start.5 = (bf16[8,112,128]{2,1,0:T(8,128)(2,1)S(1)}, bf16[8,112,128]{2,1,0:T(8,128)(2,1)S(1)}, u32[]{:S(2)}, u32[]{:S(2)}) collective-permute-start(bf16[8,112,128]{2,1,0:T(8,128)(2,1)S(1)} %get-tuple-element.7), channel_id=1, source_target_pairs={{0,128},{128,256},{256,384},{384,0},{1,129},{129,257},{257,385},{3... | collective-permute-start | bytes 688136 | tf_op jit(solution)/shard_map/ppermute | solution.py:229
  48.4 3.5 %collective-permute-start.6 = (bf16[8,112,128]{2,1,0:T(8,128)(2,1)S(1)}, bf16[8,112,128]{2,1,0:T(8,128)(2,1)S(1)}, u32[]{:S(2)}, u32[]{:S(2)}) collective-permute-start(bf16[8,112,128]{2,1,0:T(8,128)(2,1)S(1)} %get-tuple-element.8), channel_id=1, source_target_pairs={{128,0},{256,128},{384,256},{0,384},{129,1},{257,129},{385,257},{1... | collective-permute-start | bytes 688136 | tf_op jit(solution)/shard_map/ppermute | solution.py:230
  51.8 2.0 %shard_map.48.toep_ref = bf16[16,56,256]{2,1,0:T(8,128)(2,1)S(1)} custom-call(f32[16,256]{1,0:T(8,128)S(1)} %pad_convert_fusion.taps_ref), custom_call_target="tpu_custom_call" | custom-call | flops 10000000 | bytes 1000000 | tf_op jit(solution)/shard_map/pallas_call | solution.py:220
  53.8 0.6 collective-permute-done.4
  54.4 0.0 collective-permute-done.5.low_ref
  54.4 3.0 %collective-permute-done.6.high_ref = bf16[8,112,128]{2,1,0:T(8,128)(2,1)S(1)} collective-permute-done((bf16[8,112,128]{2,1,0:T(8,128)(2,1)S(1)}, bf16[8,112,128]{2,1,0:T(8,128)(2,1)S(1)}, u32[]{:S(2)}, u32[]{:S(2)}) %collective-permute-start.6) | collective-permute-done | bytes 229408 | tf_op jit(solution)/shard_map/ppermute | solution.py:230
  57.5 5.6 %shard_map.49 = bf16[32,6,16,128]{3,2,1,0:T(8,128)(2,1)} custom-call(bf16[16,32,512]{2,1,0:T(8,128)(2,1)S(1)} %constant_dynamic-update-slice_fusion.5.unused_ref.weight_ref, bf16[8,112,128]{2,1,0:T(8,128)(2,1)S(1)} %collective-permute-done.5.low_ref, bf16[8,8,48,128]{3,2,1,0:T(8,128)(2,1)S(1)} %all-to-all-done.run_ref.mid_ref, ...), custom_call_target="tpu_custom_call" | custom-call | flops 1000000000 | bytes 3000000 | tf_op jit(solution)/shard_map/pallas_call | solution.py:232
  63.0 8.4 %all-to-all-start.1 = ((bf16[32,6,16,128]{3,2,1,0:T(8,128)(2,1)}), bf16[32,6,16,128]{3,2,1,0:T(8,128)(2,1)S(1)}, u32[]{:S(2)}, u32[]{:S(2)}) async-start(bf16[32,6,16,128]{3,2,1,0:T(8,128)(2,1)} %shard_map.49), calls=%async_computation.1 | async-start | bytes 1572864 | tf_op jit(solution)/shard_map/all_to_all | solution.py:242
  71.5 25.6 %all-to-all-done.1.hidden_ref = bf16[32,6,16,128]{3,2,1,0:T(8,128)(2,1)S(1)} async-done(((bf16[32,6,16,128]{3,2,1,0:T(8,128)(2,1)}), bf16[32,6,16,128]{3,2,1,0:T(8,128)(2,1)S(1)}, u32[]{:S(2)}, u32[]{:S(2)}) %all-to-all-start.1) | async-done | bytes 786464 | tf_op jit(solution)/shard_map/all_to_all | solution.py:242
  97.1 1.2 shard_map.50
  98.3 0.0 copy-start.2
  98.3 30.0 %all_to_all.15 = bf16[64,3,16,128]{3,2,1,0:T(8,128)(2,1)S(1)} all-to-all(bf16[64,3,16,128]{3,2,1,0:T(8,128)(2,1)S(1)} %bitcast.11), channel_id=1, replica_groups=mesh['x'=4,'zl'=4,'core'=2,'zh'=2,'y'=8] {'zl','zh','y'}, dimensions={0} | all-to-all | bytes 1572864 | tf_op jit(solution)/shard_map/all_to_all | solution.py:249
  128.3 1.3 shard_map.51
  (19 shorter events, 0.2 us)
Async XLA Ops:
  0.0 45.0 %copy-start = (bf16[32,16,3,3]{0,1,3,2:T(8,128)(2,1)S(1)}, bf16[32,16,3,3]{0,1,3,2:T(8,128)(2,1)}, u32[]{:S(2)}) copy-start(bf16[32,16,3,3]{0,1,3,2:T(8,128)(2,1)} %param.6) | copy-start | bytes 27652
  0.0 1.1 copy-start.1
  3.1 7.4 %copy-start.3 = (bf16[32,512]{1,0:T(8,128)(2,1)S(1)}, bf16[32,512]{1,0:T(8,128)(2,1)}, u32[]{:S(2)}) copy-start(bf16[32,512]{1,0:T(8,128)(2,1)} %param.7) | copy-start | bytes 98308
  3.1 42.8 %all-to-all-start = ((bf16[8,8,48,128]{3,2,1,0:T(8,128)(2,1)}), bf16[8,8,48,128]{3,2,1,0:T(8,128)(2,1)S(1)}, u32[]{:S(2)}, u32[]{:S(2)}) async-start(bf16[8,8,48,128]{3,2,1,0:T(8,128)(2,1)} %bitcast.4), calls=%async_computation | async-start | bytes 1572864 | tf_op jit(solution)/shard_map/all_to_all | solution.py:215
  10.7 14.5 %collective-permute-start.2 = (bf16[1,32,512]{2,1,0:T(8,128)(2,1)S(1)}, bf16[1,32,512]{2,1,0:T(8,128)(2,1)S(1)}, u32[]{:S(2)}, u32[]{:S(2)}) collective-permute-start(bf16[1,32,512]{2,1,0:T(8,128)(2,1)S(1)} %copy.14), channel_id=1, source_target_pairs={{0,6},{1,7},{2,0},{3,1},{4,2},{5,3},{6,4},{7,5},{8,14},{9,15},{10,... | collective-permute-start | bytes 98312 | tf_op jit(solution)/shard_map/ppermute | solution.py:189
  16.9 9.7 %collective-permute-start.1 = (bf16[1,32,512]{2,1,0:T(8,128)(2,1)S(1)}, bf16[1,32,512]{2,1,0:T(8,128)(2,1)S(1)}, u32[]{:S(2)}, u32[]{:S(2)}) collective-permute-start(bf16[1,32,512]{2,1,0:T(8,128)(2,1)S(1)} %copy.14), channel_id=1, source_target_pairs={{0,4},{1,5},{2,6},{3,7},{4,0},{5,1},{6,2},{7,3},{8,12},{9,13},{10,... | collective-permute-start | bytes 98312 | tf_op jit(solution)/shard_map/ppermute | solution.py:189
  20.7 7.9 %collective-permute-start = (bf16[1,32,512]{2,1,0:T(8,128)(2,1)S(1)}, bf16[1,32,512]{2,1,0:T(8,128)(2,1)S(1)}, u32[]{:S(2)}, u32[]{:S(2)}) collective-permute-start(bf16[1,32,512]{2,1,0:T(8,128)(2,1)S(1)} %copy.14), channel_id=1, source_target_pairs={{0,2},{1,3},{2,4},{3,5},{4,6},{5,7},{6,0},{7,1},{8,10},{9,11},{10,... | collective-permute-start | bytes 98312 | tf_op jit(solution)/shard_map/ppermute | solution.py:189
  28.7 8.1 %collective-permute-start.3 = (bf16[4,32,512]{2,1,0:T(8,128)(2,1)S(1)}, bf16[4,32,512]{2,1,0:T(8,128)(2,1)S(1)}, u32[]{:S(2)}, u32[]{:S(2)}) collective-permute-start(bf16[4,32,512]{2,1,0:T(8,128)(2,1)S(1)} %pad_maximum_fusion), channel_id=1, source_target_pairs={{0,1},{1,2},{2,3},{3,4},{4,5},{5,6},{6,7},{7,0},{8,9},{9,10},{10,1... | collective-permute-start | bytes 393224 | tf_op jit(solution)/shard_map/ppermute | solution.py:189
  36.8 17.6 %collective-permute-start.4 = (bf16[8,32,512]{2,1,0:T(8,128)(2,1)S(1)}, bf16[8,32,512]{2,1,0:T(8,128)(2,1)S(1)}, u32[]{:S(2)}, u32[]{:S(2)}) collective-permute-start(bf16[8,32,512]{2,1,0:T(8,128)(2,1)S(1)} %get-tuple-element.9.unused_ref), channel_id=1, source_target_pairs={{0,8},{8,0},{1,9},{9,1},{2,10},{10,2},{3,11},{11,3},{4,12},{12,4},... | collective-permute-start | bytes 786440 | tf_op jit(solution)/shard_map/ppermute | solution.py:189
  45.2 0.7 copy-start.4
  46.0 8.5 %collective-permute-start.5 = (bf16[8,112,128]{2,1,0:T(8,128)(2,1)S(1)}, bf16[8,112,128]{2,1,0:T(8,128)(2,1)S(1)}, u32[]{:S(2)}, u32[]{:S(2)}) collective-permute-start(bf16[8,112,128]{2,1,0:T(8,128)(2,1)S(1)} %get-tuple-element.7), channel_id=1, source_target_pairs={{0,128},{128,256},{256,384},{384,0},{1,129},{129,257},{257,385},{3... | collective-permute-start | bytes 688136 | tf_op jit(solution)/shard_map/ppermute | solution.py:229
  48.4 9.1 %collective-permute-start.6 = (bf16[8,112,128]{2,1,0:T(8,128)(2,1)S(1)}, bf16[8,112,128]{2,1,0:T(8,128)(2,1)S(1)}, u32[]{:S(2)}, u32[]{:S(2)}) collective-permute-start(bf16[8,112,128]{2,1,0:T(8,128)(2,1)S(1)} %get-tuple-element.8), channel_id=1, source_target_pairs={{128,0},{256,128},{384,256},{0,384},{129,1},{257,129},{385,257},{1... | collective-permute-start | bytes 688136 | tf_op jit(solution)/shard_map/ppermute | solution.py:230
  63.0 34.0 %all-to-all-start.1 = ((bf16[32,6,16,128]{3,2,1,0:T(8,128)(2,1)}), bf16[32,6,16,128]{3,2,1,0:T(8,128)(2,1)S(1)}, u32[]{:S(2)}, u32[]{:S(2)}) async-start(bf16[32,6,16,128]{3,2,1,0:T(8,128)(2,1)} %shard_map.49), calls=%async_computation.1 | async-start | bytes 1572864 | tf_op jit(solution)/shard_map/all_to_all | solution.py:242
  98.3 30.0 %copy-start.2 = (bf16[2,32,45,128]{3,1,2,0:T(8,128)(2,1)S(1)}, bf16[2,32,45,128]{3,1,2,0:T(8,128)(2,1)}, u32[]{:S(2)}) copy-start(bf16[2,32,45,128]{3,1,2,0:T(8,128)(2,1)} %param.4) | copy-start | bytes 2211844

commit v3 on v2

--- a/solution.py
+++ b/solution.py
@@ -57,7 +57,7 @@
     return jnp.concatenate([v[:, 64:], v[:, :64]], axis=1)
 
 
-def rim_kernel(run_ref, unused_ref, low_ref, high_ref):
+def rim_kernel(run_ref, low_ref, high_ref):
     low_ref[:, 0:16] = run_ref[5, :, 32:48]
     low_ref[:, 16:64] = run_ref[6]
     low_ref[:, 64:112] = run_ref[7]
@@ -66,7 +66,7 @@
     high_ref[:, 96:112] = run_ref[2, :, 0:16]
 
 
-def conv_kernel(unused_ref, low_ref, mid_ref, high_ref, toep_ref, weight_ref, out_ref, zonal, shifted):
+def zonal_kernel(low_ref, mid_ref, high_ref, toep_ref, zonal):
     lane = lax.broadcasted_iota(jnp.int32, (SLOT, 128), 1)
     first_half = lane < 64
     tile_row = lax.broadcasted_iota(jnp.int32, (16, 128), 0)
@@ -96,26 +96,36 @@
 
             wide = {b: paired(blocks, blocks_turned, b) for b in range(-2, 6)}
             taps = toep_ref[part * 8 + c]
+            windows = []
             for b in range(4):
                 rim = jnp.where(
                     tile_row >= 8,
                     paired(tails, tails_turned, b - 3),
                     paired(heads, heads_turned, b + 3),
                 )
-                window = jnp.concatenate([wide[b + k] for k in range(-2, 3)] + [rim], axis=0)
+                windows.append(
+                    jnp.concatenate([wide[b + k] for k in range(-2, 3)] + [rim], axis=0)
+                )
+            for b in (0, 2):
+                window = jnp.concatenate(windows[b : b + 2], axis=1)
                 result = jnp.dot(taps, window, preferred_element_type=F32)
-                zonal[pl.ds(b * TALL * GROUP + part * 8 + c, TALL, stride=GROUP), :] = result
+                for k in range(2):
+                    first = (b + k) * TALL * GROUP + part * 8 + c
+                    zonal[pl.ds(first, TALL, stride=GROUP), :] = result[:, k * 128 : k * 128 + 128]
 
     for c in range(8):
         one_pair(c)
 
+
+def conv_kernel(unused_ref, zonal, weight_ref, out_ref, shifted):
     place = lax.broadcasted_iota(jnp.int32, (TALL * GROUP, 128), 1) % 64
     for b in range(4):
-        z = zonal[b * TALL * GROUP : (b + 1) * TALL * GROUP, :]
-        south = jnp.where(place < 2, 0.0, pltpu.roll(z, 2, 1))
-        north = jnp.where(place >= 62, 0.0, pltpu.roll(z, 126, 1))
+        z = zonal[b * TALL * GROUP : (b + 1) * TALL * GROUP, :].astype(BF16)
+        zero = jnp.zeros_like(z)
+        south = jnp.where(place < 2, zero, jnp.concatenate([z[:, 126:], z[:, :126]], axis=1))
+        north = jnp.where(place >= 62, zero, jnp.concatenate([z[:, 2:], z[:, :2]], axis=1))
         for a, v in enumerate((south, z, north)):
-            shifted[b, a] = v.astype(BF16).reshape(TALL, GROUP, 128)
+            shifted[b, a] = v.reshape(TALL, GROUP, 128)
 
     weight = weight_ref[...]
 
@@ -182,18 +192,16 @@
     )
 
 
-def with_behind(blocks, axis, *steps):
+def from_behind(blocks, axis, step):
     count = lax.axis_size(axis)
-    parts = [blocks]
-    for step in steps:
-        parts.append(lax.ppermute(blocks, axis, [(i, (i + step) % count) for i in range(count)]))
-    return jnp.concatenate(parts, axis=0)
+    return lax.ppermute(blocks, axis, [(i, (i + step) % count) for i in range(count)])
 
 
 def block_owners():
     i = jnp.arange(16)
+    i = jnp.where(i < 8, i, 8 + (i + 4 * lax.axis_index("core")) % 8)
     zh = (lax.axis_index("zh") + i // 8) % 2
-    y = (lax.axis_index("y") - 2 * (i % 4) - i // 4 % 2) % 8
+    y = (lax.axis_index("y") - 4 + i) % 8
     return (zh * 8 + y).astype(jnp.int32)
 
 
@@ -202,8 +210,13 @@
     vmem = pl.BlockSpec(memory_space=pltpu.VMEM)
     loose = pl.BlockSpec(memory_space=pl.ANY)
     by_group = mix_weight.reshape(CHANS, 16, 2, GROUP).transpose(0, 2, 1, 3).reshape(CHANS, 512)
-    few = with_behind(with_behind(by_group[None], "y", 2, 4, 6), "y", 1)
-    mix_full = with_behind(few, "zh", 1)
+    few = by_group[None]
+    few = jnp.concatenate([from_behind(few, "y", 1), few, from_behind(few, "y", -1)], axis=0)
+    few = jnp.concatenate(
+        [from_behind(few, "y", 3), few, from_behind(few[:2], "y", -3)], axis=0
+    )
+    half = from_behind(lax.dynamic_slice_in_dim(few, 4 * core, 4, 0), "zh", 1)
+    mix_full = jnp.concatenate([few, half, from_behind(half, "core", 1)], axis=0)
 
     columns = fields.transpose(0, 2, 1, 3)
     units = kernel_call(
@@ -225,20 +238,21 @@
     east = [(i, (i + 1) % count) for i in range(count)]
     west = [(b, a) for a, b in east]
     rim = jax.ShapeDtypeStruct((8, 112, 128), BF16)
-    low, high = kernel_call(rim_kernel, [rim, rim], in_specs=[vmem, loose], cost=(0, 10**6))(run, few)
+    low, high = kernel_call(rim_kernel, [rim, rim], cost=(0, 10**6))(run)
     low = lax.ppermute(low, "x", east)
     high = lax.ppermute(high, "x", west)
 
+    zonal_shape = [jax.ShapeDtypeStruct((4 * TALL * GROUP, 128), F32)]
+    zonal = kernel_call(zonal_kernel, zonal_shape, cost=(10**9, 3 * 10**6))(
+        low, run, high, toeplitz
+    )[0]
     hidden = kernel_call(
         conv_kernel,
         (32, 6, GROUP, 128),
-        scratch=(
-            pltpu.VMEM((4 * TALL * GROUP, 128), F32),
-            pltpu.VMEM((4, 3, TALL, GROUP, 128), BF16),
-        ),
+        scratch=(pltpu.VMEM((4, 3, TALL, GROUP, 128), BF16),),
         cost=(10**9, 3 * 10**6),
-        in_specs=[loose] + [vmem] * 5,
-    )(mix_full, low, run, high, toeplitz, weight)
+        in_specs=[loose, vmem, vmem],
+    )(half, zonal, weight)
     gathered = lax.all_to_all(hidden, ("core", "zh", "y"), 0, 0, tiled=True)
     mixed = kernel_call(
         mix_kernel,

time: 131 us -> 129 us (0.985); the launches traced: 130 us -> 126 us
  waiting for transfers between devices: 36.9 us -> 31.5 us
  starting transfers between devices: 48.1 us -> 50.3 us
    ppermute x1, waiting for transfers between devices: 3.04 us -> 0.01 us  [per_device(): high = lax.ppermute(high, 'x', west)]
    all_to_all x1, waiting for transfers between devices: 25.6 us -> 22.5 us  [per_device(): gathered = lax.all_to_all(hidden, ('core', 'zh', 'y'), 0, 0, tiled=True)]
    all_to_all x1, starting transfers between devices: 8.45 us -> 10.7 us  [per_device(): gathered = lax.all_to_all(hidden, ('core', 'zh', 'y'), 0, 0, tiled=True)]
    ppermute x5 -> x6, waiting for transfers between devices: 8.25 us -> 8.99 us  [from_behind(): lax.ppermute(blocks, axis, [(i, (i + step) % count) for i in range(count)])]
    pallas_call x2 -> x3, Pallas kernels: 5.6 us -> 5.77 us  [the longest x1 4.23 us: per_device(): kernel_call(conv_kernel, (32, 6, GROUP, 128), scratch=(pltpu.VMEM((4, 3,...]
    ppermute x5 -> x6, starting transfers between devices: 26.4 us -> 26.6 us  [from_behind(): lax.ppermute(blocks, axis, [(i, (i + step) % count) for i in range(count)])]
  transfers between devices with their start and end apart: 9 -> 10, of which waited for: 6 -> 5; matrix products, arithmetic and copies ran while one was open for 0% -> 1% of each run, Pallas kernels for 2% -> 3%
where the time goes in v3:
time: 129 us; the launch traced here: 126 us
  starting transfers between devices  50.3 us (39%)
  waiting for transfers between devices  31.5 us (24%)
  blocking collectives  30 us (23%)
  Pallas kernels  12.2 us (9%)
  local copies, waits for them, and re-layouts  1.74 us (1%)
    all_to_all x1, blocking collectives, per_device(): lax.all_to_all(mixed.reshape(64, 3, GROUP, 128), ('zl', 'zh', 'y'), 0, 0,...  30 us
    ppermute x6, starting transfers between devices, from_behind(): lax.ppermute(blocks, axis, [(i, (i + step) % count) for i in range(count)])  26.6 us
    all_to_all x1, waiting for transfers between devices, per_device(): gathered = lax.all_to_all(hidden, ('core', 'zh', 'y'), 0, 0, tiled=True)  22.5 us
    all_to_all x1, starting transfers between devices, per_device(): gathered = lax.all_to_all(hidden, ('core', 'zh', 'y'), 0, 0, tiled=True)  10.7 us
    ppermute x6, waiting for transfers between devices, from_behind(): lax.ppermute(blocks, axis, [(i, (i + step) % count) for i in range(count)])  8.99 us
    all_to_all x1, starting transfers between devices, per_device(): lax.all_to_all(units.reshape(BLOCKS, 8, SLOT, 128), ('zl', 'core'), 0, 0,...  7.27 us
    pallas_call x1, Pallas kernels, per_device(): kernel_call(conv_kernel, (32, 6, GROUP, 128), scratch=(pltpu.VMEM((4, 3,...  4.23 us
    ppermute x1, starting transfers between devices, per_device(): high = lax.ppermute(high, 'x', west)  3.92 us
  transfers between devices with their start and end apart: 10, of which 5 were waited for; matrix products, arithmetic and copies ran while one was open for 1% of the time, Pallas kernels for 3%

profile of v3, /device:TPU:6, one launch (start us, length us, event | category | flops | bytes accessed | tf_op | source)
XLA Modules:
  0.0 126.2 jit_solution(12744406356210574672)
XLA Ops:
  0.0 1.1 copy-done.1
  1.1 2.0 %shard_map.46 = bf16[2,2,2,8,48,128]{5,4,3,2,1,0:T(8,128)(2,1)} custom-call(bf16[2,45,32,128]{3,2,1,0:T(8,128)(2,1)S(1)} %bitcast.13), custom_call_target="tpu_custom_call" | custom-call | flops 200000000 | bytes 3000000 | tf_op jit(solution)/shard_map/pallas_call | solution.py:222
  3.1 7.3 %all-to-all-start = ((bf16[8,8,48,128]{3,2,1,0:T(8,128)(2,1)}), bf16[8,8,48,128]{3,2,1,0:T(8,128)(2,1)S(1)}, u32[]{:S(2)}, u32[]{:S(2)}) async-start(bf16[8,8,48,128]{3,2,1,0:T(8,128)(2,1)} %bitcast.4), calls=%async_computation | async-start | bytes 1572864 | tf_op jit(solution)/shard_map/all_to_all | solution.py:228
  10.4 0.1 copy.7
  10.5 0.1 copy.9
  10.6 5.4 %collective-permute-start.1 = (bf16[1,32,512]{2,1,0:T(8,128)(2,1)S(1)}, bf16[1,32,512]{2,1,0:T(8,128)(2,1)S(1)}, u32[]{:S(2)}, u32[]{:S(2)}) collective-permute-start(bf16[1,32,512]{2,1,0:T(8,128)(2,1)S(1)} %copy.9), channel_id=1, source_target_pairs={{0,7},{1,0},{2,1},{3,2},{4,3},{5,4},{6,5},{7,6},{8,15},{9,8},{10,9... | collective-permute-start | bytes 98312 | tf_op jit(solution)/shard_map/ppermute | solution.py:197
  16.0 1.9 %collective-permute-start = (bf16[1,32,512]{2,1,0:T(8,128)(2,1)S(1)}, bf16[1,32,512]{2,1,0:T(8,128)(2,1)S(1)}, u32[]{:S(2)}, u32[]{:S(2)}) collective-permute-start(bf16[1,32,512]{2,1,0:T(8,128)(2,1)S(1)} %copy.9), channel_id=1, source_target_pairs={{0,1},{1,2},{2,3},{3,4},{4,5},{5,6},{6,7},{7,0},{8,9},{9,10},{10,1... | collective-permute-start | bytes 98312 | tf_op jit(solution)/shard_map/ppermute | solution.py:197
  18.0 0.1 dynamic-slice_bitcast_fusion
  18.1 5.0 %collective-permute-done = bf16[1,32,512]{2,1,0:T(8,128)(2,1)S(1)} collective-permute-done((bf16[1,32,512]{2,1,0:T(8,128)(2,1)S(1)}, bf16[1,32,512]{2,1,0:T(8,128)(2,1)S(1)}, u32[]{:S(2)}, u32[]{:S(2)}) %collective-permute-start) | collective-permute-done | bytes 32800 | tf_op jit(solution)/shard_map/ppermute | solution.py:197
  23.0 1.9 %collective-permute-start.2 = (bf16[3,32,512]{2,1,0:T(8,128)(2,1)S(1)}, bf16[3,32,512]{2,1,0:T(8,128)(2,1)S(1)}, u32[]{:S(2)}, u32[]{:S(2)}) collective-permute-start(bf16[3,32,512]{2,1,0:T(8,128)(2,1)S(1)} %pad_maximum_fusion), channel_id=1, source_target_pairs={{0,3},{1,4},{2,5},{3,6},{4,7},{5,0},{6,1},{7,2},{8,11},{9,12},{10,... | collective-permute-start | bytes 294920 | tf_op jit(solution)/shard_map/ppermute | solution.py:197
  25.0 6.9 %collective-permute-start.3 = (bf16[2,32,512]{2,1,0:T(8,128)(2,1)S(1)}, bf16[2,32,512]{2,1,0:T(8,128)(2,1)S(1)}, u32[]{:S(2)}, u32[]{:S(2)}) collective-permute-start(bf16[2,32,512]{2,1,0:T(8,128)(2,1)S(1)} %pad_maximum_fusion.1), channel_id=1, source_target_pairs={{0,5},{1,6},{2,7},{3,0},{4,1},{5,2},{6,3},{7,4},{8,13},{9,14},{10,... | collective-permute-start | bytes 196616 | tf_op jit(solution)/shard_map/ppermute | solution.py:197
  31.9 2.4 %collective-permute-done.2 = bf16[3,32,512]{2,1,0:T(8,128)(2,1)S(1)} collective-permute-done((bf16[3,32,512]{2,1,0:T(8,128)(2,1)S(1)}, bf16[3,32,512]{2,1,0:T(8,128)(2,1)S(1)}, u32[]{:S(2)}, u32[]{:S(2)}) %collective-permute-start.2) | collective-permute-done | bytes 98336 | tf_op jit(solution)/shard_map/ppermute | solution.py:197
  34.4 0.0 all-to-all-done.run_ref.mid_ref
  34.5 1.9 %collective-permute-start.6 = (bf16[8,112,128]{2,1,0:T(8,128)(2,1)S(1)}, bf16[8,112,128]{2,1,0:T(8,128)(2,1)S(1)}, u32[]{:S(2)}, u32[]{:S(2)}) collective-permute-start(bf16[8,112,128]{2,1,0:T(8,128)(2,1)S(1)} %get-tuple-element.7), channel_id=1, source_target_pairs={{0,128},{128,256},{256,384},{384,0},{1,129},{129,257},{257,385},{3... | collective-permute-start | bytes 688136 | tf_op jit(solution)/shard_map/ppermute | solution.py:242
  36.4 3.9 %collective-permute-start.7 = (bf16[8,112,128]{2,1,0:T(8,128)(2,1)S(1)}, bf16[8,112,128]{2,1,0:T(8,128)(2,1)S(1)}, u32[]{:S(2)}, u32[]{:S(2)}) collective-permute-start(bf16[8,112,128]{2,1,0:T(8,128)(2,1)S(1)} %get-tuple-element.8), channel_id=1, source_target_pairs={{128,0},{256,128},{384,256},{0,384},{129,1},{257,129},{385,257},{1... | collective-permute-start | bytes 688136 | tf_op jit(solution)/shard_map/ppermute | solution.py:243
  40.4 8.2 %collective-permute-start.4 = (bf16[4,32,512]{2,1,0:T(8,128)(2,1)S(1)}, bf16[4,32,512]{2,1,0:T(8,128)(2,1)S(1)}, u32[]{:S(2)}, u32[]{:S(2)}) collective-permute-start(bf16[4,32,512]{2,1,0:T(8,128)(2,1)S(1)} %constant_dynamic-slice_fusion.1), channel_id=1, source_target_pairs={{0,8},{8,0},{1,9},{9,1},{2,10},{10,2},{3,11},{11,3},{4,12},{12,4},... | collective-permute-start | bytes 393224 | tf_op jit(solution)/shard_map/ppermute | solution.py:197
  48.6 0.1 copy.15
  48.8 0.1 reshape.17.weight_ref
  48.8 2.0 %shard_map.48.toep_ref = bf16[16,56,256]{2,1,0:T(8,128)(2,1)S(1)} custom-call(f32[16,256]{1,0:T(8,128)S(1)} %pad_convert_fusion.taps_ref), custom_call_target="tpu_custom_call" | custom-call | flops 10000000 | bytes 1000000 | tf_op jit(solution)/shard_map/pallas_call | solution.py:233
  50.9 0.0 collective-permute-done.6.low_ref
  50.9 0.0 collective-permute-done.7.high_ref
  50.9 1.5 %shard_map.49.zonal = f32[3584,128]{1,0:T(8,128)S(1)} custom-call(bf16[8,112,128]{2,1,0:T(8,128)(2,1)S(1)} %collective-permute-done.6.low_ref, bf16[8,8,48,128]{3,2,1,0:T(8,128)(2,1)S(1)} %all-to-all-done.run_ref.mid_ref, bf16[8,112,128]{2,1,0:T(8,128)(2,1)S(1)} %collective-permute-done.7.high_ref, bf16[16,56,256]{2,1,0:T(8,128)(2,1)S(1)} %shard_map.48.toep_ref), custom_call_target="tpu_custom_call" | custom-call | flops 1000000000 | bytes 3000000 | tf_op jit(solution)/shard_map/pallas_call | solution.py:246
  52.4 0.6 collective-permute-done.4.unused_ref
  53.0 4.2 %shard_map.50 = bf16[32,6,16,128]{3,2,1,0:T(8,128)(2,1)} custom-call(bf16[4,32,512]{2,1,0:T(8,128)(2,1)S(1)} %collective-permute-done.4.unused_ref, f32[3584,128]{1,0:T(8,128)S(1)} %shard_map.49.zonal, bf16[16,144]{1,0:T(8,128)(2,1)S(1)} %reshape.17.weight_ref), custom_call_target="tpu_custom_call" | custom-call | flops 1000000000 | bytes 3000000 | tf_op jit(solution)/shard_map/pallas_call | solution.py:249
  57.2 10.7 %all-to-all-start.1 = ((bf16[32,6,16,128]{3,2,1,0:T(8,128)(2,1)}), bf16[32,6,16,128]{3,2,1,0:T(8,128)(2,1)S(1)}, u32[]{:S(2)}, u32[]{:S(2)}) async-start(bf16[32,6,16,128]{3,2,1,0:T(8,128)(2,1)} %shard_map.50), calls=%async_computation.1 | async-start | bytes 1572864 | tf_op jit(solution)/shard_map/all_to_all | solution.py:256
  67.9 2.2 %collective-permute-start.5 = (bf16[4,32,512]{2,1,0:T(8,128)(2,1)S(1)}, bf16[4,32,512]{2,1,0:T(8,128)(2,1)S(1)}, u32[]{:S(2)}, u32[]{:S(2)}) collective-permute-start(bf16[4,32,512]{2,1,0:T(8,128)(2,1)S(1)} %collective-permute-done.4.unused_ref), channel_id=1, source_target_pairs={{0,16},{16,0},{1,17},{17,1},{2,18},{18,2},{3,19},{19,3},{4,20},{20... | collective-permute-start | bytes 393224 | tf_op jit(solution)/shard_map/ppermute | solution.py:197
  70.1 1.0 collective-permute-done.5
  71.1 0.0 copy-start.2
  71.2 22.5 %all-to-all-done.1.hidden_ref = bf16[32,6,16,128]{3,2,1,0:T(8,128)(2,1)S(1)} async-done(((bf16[32,6,16,128]{3,2,1,0:T(8,128)(2,1)}), bf16[32,6,16,128]{3,2,1,0:T(8,128)(2,1)S(1)}, u32[]{:S(2)}, u32[]{:S(2)}) %all-to-all-start.1) | async-done | bytes 786464 | tf_op jit(solution)/shard_map/all_to_all | solution.py:256
  93.7 1.2 shard_map.51
  94.9 30.0 %all_to_all.15 = bf16[64,3,16,128]{3,2,1,0:T(8,128)(2,1)S(1)} all-to-all(bf16[64,3,16,128]{3,2,1,0:T(8,128)(2,1)S(1)} %bitcast.11), channel_id=1, replica_groups=mesh['x'=4,'zl'=4,'core'=2,'zh'=2,'y'=8] {'zl','zh','y'}, dimensions={0} | all-to-all | bytes 1572864 | tf_op jit(solution)/shard_map/all_to_all | solution.py:263
  124.9 1.3 %shard_map.52 = bf16[2,45,32,128]{3,2,1,0:T(8,128)(2,1)} custom-call(bf16[2,2,48,16,128]{4,3,2,1,0:T(8,128)(2,1)S(1)} %bitcast.12, bf16[2,45,32,128]{3,2,1,0:T(8,128)(2,1)S(1)} %bitcast.14), custom_call_target="tpu_custom_call" | custom-call | flops 200000000 | bytes 3000000 | tf_op jit(solution)/shard_map/pallas_call | solution.py:264
  (25 shorter events, 0.2 us)
Async XLA Ops:
  0.0 17.9 %copy-start = (bf16[32,16,3,3]{0,1,3,2:T(8,128)(2,1)S(1)}, bf16[32,16,3,3]{0,1,3,2:T(8,128)(2,1)}, u32[]{:S(2)}) copy-start(bf16[32,16,3,3]{0,1,3,2:T(8,128)(2,1)} %param.6) | copy-start | bytes 27652
  0.0 1.1 copy-start.1
  1.1 9.3 %copy-start.3 = (bf16[32,512]{1,0:T(8,128)(2,1)S(1)}, bf16[32,512]{1,0:T(8,128)(2,1)}, u32[]{:S(2)}) copy-start(bf16[32,512]{1,0:T(8,128)(2,1)} %param.7) | copy-start | bytes 98308
  1.1 16.9 %copy-start.4 = (bf16[32,181]{1,0:T(8,128)(2,1)S(1)}, bf16[32,181]{1,0:T(8,128)(2,1)}, u32[]{:S(2)}) copy-start(bf16[32,181]{1,0:T(8,128)(2,1)} %param.5) | copy-start | bytes 34756
  3.1 31.3 %all-to-all-start = ((bf16[8,8,48,128]{3,2,1,0:T(8,128)(2,1)}), bf16[8,8,48,128]{3,2,1,0:T(8,128)(2,1)S(1)}, u32[]{:S(2)}, u32[]{:S(2)}) async-start(bf16[8,8,48,128]{3,2,1,0:T(8,128)(2,1)} %bitcast.4), calls=%async_computation | async-start | bytes 1572864 | tf_op jit(solution)/shard_map/all_to_all | solution.py:228
  10.6 7.4 %collective-permute-start.1 = (bf16[1,32,512]{2,1,0:T(8,128)(2,1)S(1)}, bf16[1,32,512]{2,1,0:T(8,128)(2,1)S(1)}, u32[]{:S(2)}, u32[]{:S(2)}) collective-permute-start(bf16[1,32,512]{2,1,0:T(8,128)(2,1)S(1)} %copy.9), channel_id=1, source_target_pairs={{0,7},{1,0},{2,1},{3,2},{4,3},{5,4},{6,5},{7,6},{8,15},{9,8},{10,9... | collective-permute-start | bytes 98312 | tf_op jit(solution)/shard_map/ppermute | solution.py:197
  16.0 7.0 %collective-permute-start = (bf16[1,32,512]{2,1,0:T(8,128)(2,1)S(1)}, bf16[1,32,512]{2,1,0:T(8,128)(2,1)S(1)}, u32[]{:S(2)}, u32[]{:S(2)}) collective-permute-start(bf16[1,32,512]{2,1,0:T(8,128)(2,1)S(1)} %copy.9), channel_id=1, source_target_pairs={{0,1},{1,2},{2,3},{3,4},{4,5},{5,6},{6,7},{7,0},{8,9},{9,10},{10,1... | collective-permute-start | bytes 98312 | tf_op jit(solution)/shard_map/ppermute | solution.py:197
  23.0 11.3 %collective-permute-start.2 = (bf16[3,32,512]{2,1,0:T(8,128)(2,1)S(1)}, bf16[3,32,512]{2,1,0:T(8,128)(2,1)S(1)}, u32[]{:S(2)}, u32[]{:S(2)}) collective-permute-start(bf16[3,32,512]{2,1,0:T(8,128)(2,1)S(1)} %pad_maximum_fusion), channel_id=1, source_target_pairs={{0,3},{1,4},{2,5},{3,6},{4,7},{5,0},{6,1},{7,2},{8,11},{9,12},{10,... | collective-permute-start | bytes 294920 | tf_op jit(solution)/shard_map/ppermute | solution.py:197
  25.0 15.4 %collective-permute-start.3 = (bf16[2,32,512]{2,1,0:T(8,128)(2,1)S(1)}, bf16[2,32,512]{2,1,0:T(8,128)(2,1)S(1)}, u32[]{:S(2)}, u32[]{:S(2)}) collective-permute-start(bf16[2,32,512]{2,1,0:T(8,128)(2,1)S(1)} %pad_maximum_fusion.1), channel_id=1, source_target_pairs={{0,5},{1,6},{2,7},{3,0},{4,1},{5,2},{6,3},{7,4},{8,13},{9,14},{10,... | collective-permute-start | bytes 196616 | tf_op jit(solution)/shard_map/ppermute | solution.py:197
  34.5 16.4 %collective-permute-start.6 = (bf16[8,112,128]{2,1,0:T(8,128)(2,1)S(1)}, bf16[8,112,128]{2,1,0:T(8,128)(2,1)S(1)}, u32[]{:S(2)}, u32[]{:S(2)}) collective-permute-start(bf16[8,112,128]{2,1,0:T(8,128)(2,1)S(1)} %get-tuple-element.7), channel_id=1, source_target_pairs={{0,128},{128,256},{256,384},{384,0},{1,129},{129,257},{257,385},{3... | collective-permute-start | bytes 688136 | tf_op jit(solution)/shard_map/ppermute | solution.py:242
  36.4 14.4 %collective-permute-start.7 = (bf16[8,112,128]{2,1,0:T(8,128)(2,1)S(1)}, bf16[8,112,128]{2,1,0:T(8,128)(2,1)S(1)}, u32[]{:S(2)}, u32[]{:S(2)}) collective-permute-start(bf16[8,112,128]{2,1,0:T(8,128)(2,1)S(1)} %get-tuple-element.8), channel_id=1, source_target_pairs={{128,0},{256,128},{384,256},{0,384},{129,1},{257,129},{385,257},{1... | collective-permute-start | bytes 688136 | tf_op jit(solution)/shard_map/ppermute | solution.py:243
  40.4 12.6 %collective-permute-start.4 = (bf16[4,32,512]{2,1,0:T(8,128)(2,1)S(1)}, bf16[4,32,512]{2,1,0:T(8,128)(2,1)S(1)}, u32[]{:S(2)}, u32[]{:S(2)}) collective-permute-start(bf16[4,32,512]{2,1,0:T(8,128)(2,1)S(1)} %constant_dynamic-slice_fusion.1), channel_id=1, source_target_pairs={{0,8},{8,0},{1,9},{9,1},{2,10},{10,2},{3,11},{11,3},{4,12},{12,4},... | collective-permute-start | bytes 393224 | tf_op jit(solution)/shard_map/ppermute | solution.py:197
  57.2 36.5 %all-to-all-start.1 = ((bf16[32,6,16,128]{3,2,1,0:T(8,128)(2,1)}), bf16[32,6,16,128]{3,2,1,0:T(8,128)(2,1)S(1)}, u32[]{:S(2)}, u32[]{:S(2)}) async-start(bf16[32,6,16,128]{3,2,1,0:T(8,128)(2,1)} %shard_map.50), calls=%async_computation.1 | async-start | bytes 1572864 | tf_op jit(solution)/shard_map/all_to_all | solution.py:256
  67.9 3.2 %collective-permute-start.5 = (bf16[4,32,512]{2,1,0:T(8,128)(2,1)S(1)}, bf16[4,32,512]{2,1,0:T(8,128)(2,1)S(1)}, u32[]{:S(2)}, u32[]{:S(2)}) collective-permute-start(bf16[4,32,512]{2,1,0:T(8,128)(2,1)S(1)} %collective-permute-done.4.unused_ref), channel_id=1, source_target_pairs={{0,16},{16,0},{1,17},{17,1},{2,18},{18,2},{3,19},{19,3},{4,20},{20... | collective-permute-start | bytes 393224 | tf_op jit(solution)/shard_map/ppermute | solution.py:197
  71.1 53.8 %copy-start.2 = (bf16[2,32,45,128]{3,1,2,0:T(8,128)(2,1)S(1)}, bf16[2,32,45,128]{3,1,2,0:T(8,128)(2,1)}, u32[]{:S(2)}) copy-start(bf16[2,32,45,128]{3,1,2,0:T(8,128)(2,1)} %param.4) | copy-start | bytes 2211844

commit v4 on v3

--- a/solution.py
+++ b/solution.py
@@ -25,19 +25,18 @@
 
 def split_kernel(fields_ref, out_ref, wide):
     shuffle = lat_shuffle(False)
-    wide[...] = fields_ref[...].astype(F32).reshape(MEMBERS, WIDTH * CHANS, 128)
-    for m in range(MEMBERS):
-        for g in range(2):
-            for c in range(8):
-                sides = [
-                    wide[m, pl.ds(g * GROUP + part * 8 + c, WIDTH, stride=CHANS), :].astype(BF16)
-                    for part in range(2)
-                ]
-                both = jnp.concatenate(sides, axis=1)
-                moved = jnp.dot(both, shuffle, preferred_element_type=F32).astype(BF16)
-                for s in range(2):
-                    out_ref[m, s, g, c, 32:48] = jnp.zeros((16, 128), BF16)
-                    out_ref[m, s, g, c, 0:WIDTH] = moved[:, s * 128 : s * 128 + 128]
+    wide[...] = fields_ref[0].astype(F32).reshape(WIDTH * CHANS, 128)
+    for g in range(2):
+        for c in range(8):
+            sides = [
+                wide[pl.ds(g * GROUP + part * 8 + c, WIDTH, stride=CHANS), :].astype(BF16)
+                for part in range(2)
+            ]
+            both = jnp.concatenate(sides, axis=1)
+            moved = jnp.dot(both, shuffle, preferred_element_type=F32).astype(BF16)
+            for s in range(2):
+                out_ref[0, s, g, c, 32:48] = jnp.zeros((16, 128), BF16)
+                out_ref[0, s, g, c, 0:WIDTH] = moved[:, s * 128 : s * 128 + 128]
 
 
 def toeplitz_kernel(taps_ref, out_ref):
@@ -222,8 +221,11 @@
     units = kernel_call(
         split_kernel,
         (2, 2, 2, 8, SLOT, 128),
-        scratch=(pltpu.VMEM((MEMBERS, WIDTH * CHANS, 128), F32),),
+        scratch=(pltpu.VMEM((WIDTH * CHANS, 128), F32),),
         cost=(2 * 10**8, 3 * 10**6),
+        grid=(MEMBERS,),
+        in_specs=[pl.BlockSpec((1, WIDTH, CHANS, 128), lambda m: (m, 0, 0, 0))],
+        out_specs=pl.BlockSpec((1, 2, 2, 8, SLOT, 128), lambda m: (m, 0, 0, 0, 0, 0)),
     )(columns)
     run = lax.all_to_all(
         units.reshape(BLOCKS, 8, SLOT, 128), ("zl", "core"), 0, 0, tiled=True

time: 129 us -> 129 us (level)
  no operation moved by 1% of the time
where the time goes in v4:
time: 129 us; the launch traced here: 126 us
  starting transfers between devices  50.3 us (39%)
  waiting for transfers between devices  31.5 us (24%)
  blocking collectives  30 us (23%)
  Pallas kernels  12.2 us (9%)
  local copies, waits for them, and re-layouts  1.74 us (1%)
    all_to_all x1, blocking collectives, per_device(): lax.all_to_all(mixed.reshape(64, 3, GROUP, 128), ('zl', 'zh', 'y'), 0, 0,...  30 us
    ppermute x6, starting transfers between devices, from_behind(): lax.ppermute(blocks, axis, [(i, (i + step) % count) for i in range(count)])  26.6 us
    all_to_all x1, waiting for transfers between devices, per_device(): gathered = lax.all_to_all(hidden, ('core', 'zh', 'y'), 0, 0, tiled=True)  22.5 us
    all_to_all x1, starting transfers between devices, per_device(): gathered = lax.all_to_all(hidden, ('core', 'zh', 'y'), 0, 0, tiled=True)  10.6 us
    ppermute x6, waiting for transfers between devices, from_behind(): lax.ppermute(blocks, axis, [(i, (i + step) % count) for i in range(count)])  8.99 us
    all_to_all x1, starting transfers between devices, per_device(): lax.all_to_all(units.reshape(BLOCKS, 8, SLOT, 128), ('zl', 'core'), 0, 0,...  7.27 us
    pallas_call x1, Pallas kernels, per_device(): kernel_call(conv_kernel, (32, 6, GROUP, 128), scratch=(pltpu.VMEM((4, 3,...  4.23 us
    ppermute x1, starting transfers between devices, per_device(): high = lax.ppermute(high, 'x', west)  3.92 us
  transfers between devices with their start and end apart: 10, of which 5 were waited for; matrix products, arithmetic and copies ran while one was open for 1% of the time, Pallas kernels for 3%

profile of v4, /device:TPU:6, one launch (start us, length us, event | category | flops | bytes accessed | tf_op | source)
XLA Modules:
  0.0 126.2 jit_solution(15657462264532138069)
XLA Ops:
  0.0 1.1 copy-done.1
  1.1 2.0 %shard_map.46 = bf16[2,2,2,8,48,128]{5,4,3,2,1,0:T(8,128)(2,1)} custom-call(bf16[2,45,32,128]{3,2,1,0:T(8,128)(2,1)S(1)} %bitcast.13), custom_call_target="tpu_custom_call" | custom-call | flops 200000000 | bytes 3000000 | tf_op jit(solution)/shard_map/pallas_call | solution.py:221
  3.1 7.3 %all-to-all-start = ((bf16[8,8,48,128]{3,2,1,0:T(8,128)(2,1)}), bf16[8,8,48,128]{3,2,1,0:T(8,128)(2,1)S(1)}, u32[]{:S(2)}, u32[]{:S(2)}) async-start(bf16[8,8,48,128]{3,2,1,0:T(8,128)(2,1)} %bitcast.4), calls=%async_computation | async-start | bytes 1572864 | tf_op jit(solution)/shard_map/all_to_all | solution.py:230
  10.4 0.1 copy.7
  10.5 0.1 copy.9
  10.6 5.4 %collective-permute-start.1 = (bf16[1,32,512]{2,1,0:T(8,128)(2,1)S(1)}, bf16[1,32,512]{2,1,0:T(8,128)(2,1)S(1)}, u32[]{:S(2)}, u32[]{:S(2)}) collective-permute-start(bf16[1,32,512]{2,1,0:T(8,128)(2,1)S(1)} %copy.9), channel_id=1, source_target_pairs={{0,7},{1,0},{2,1},{3,2},{4,3},{5,4},{6,5},{7,6},{8,15},{9,8},{10,9... | collective-permute-start | bytes 98312 | tf_op jit(solution)/shard_map/ppermute | solution.py:196
  16.0 1.9 %collective-permute-start = (bf16[1,32,512]{2,1,0:T(8,128)(2,1)S(1)}, bf16[1,32,512]{2,1,0:T(8,128)(2,1)S(1)}, u32[]{:S(2)}, u32[]{:S(2)}) collective-permute-start(bf16[1,32,512]{2,1,0:T(8,128)(2,1)S(1)} %copy.9), channel_id=1, source_target_pairs={{0,1},{1,2},{2,3},{3,4},{4,5},{5,6},{6,7},{7,0},{8,9},{9,10},{10,1... | collective-permute-start | bytes 98312 | tf_op jit(solution)/shard_map/ppermute | solution.py:196
  18.0 0.1 dynamic-slice_bitcast_fusion
  18.1 0.0 collective-permute-done.1
  18.1 5.0 %collective-permute-done = bf16[1,32,512]{2,1,0:T(8,128)(2,1)S(1)} collective-permute-done((bf16[1,32,512]{2,1,0:T(8,128)(2,1)S(1)}, bf16[1,32,512]{2,1,0:T(8,128)(2,1)S(1)}, u32[]{:S(2)}, u32[]{:S(2)}) %collective-permute-start) | collective-permute-done | bytes 32800 | tf_op jit(solution)/shard_map/ppermute | solution.py:196
  23.0 1.9 %collective-permute-start.2 = (bf16[3,32,512]{2,1,0:T(8,128)(2,1)S(1)}, bf16[3,32,512]{2,1,0:T(8,128)(2,1)S(1)}, u32[]{:S(2)}, u32[]{:S(2)}) collective-permute-start(bf16[3,32,512]{2,1,0:T(8,128)(2,1)S(1)} %pad_maximum_fusion), channel_id=1, source_target_pairs={{0,3},{1,4},{2,5},{3,6},{4,7},{5,0},{6,1},{7,2},{8,11},{9,12},{10,... | collective-permute-start | bytes 294920 | tf_op jit(solution)/shard_map/ppermute | solution.py:196
  25.0 6.9 %collective-permute-start.3 = (bf16[2,32,512]{2,1,0:T(8,128)(2,1)S(1)}, bf16[2,32,512]{2,1,0:T(8,128)(2,1)S(1)}, u32[]{:S(2)}, u32[]{:S(2)}) collective-permute-start(bf16[2,32,512]{2,1,0:T(8,128)(2,1)S(1)} %pad_maximum_fusion.1), channel_id=1, source_target_pairs={{0,5},{1,6},{2,7},{3,0},{4,1},{5,2},{6,3},{7,4},{8,13},{9,14},{10,... | collective-permute-start | bytes 196616 | tf_op jit(solution)/shard_map/ppermute | solution.py:196
  31.9 2.4 %collective-permute-done.2 = bf16[3,32,512]{2,1,0:T(8,128)(2,1)S(1)} collective-permute-done((bf16[3,32,512]{2,1,0:T(8,128)(2,1)S(1)}, bf16[3,32,512]{2,1,0:T(8,128)(2,1)S(1)}, u32[]{:S(2)}, u32[]{:S(2)}) %collective-permute-start.2) | collective-permute-done | bytes 98336 | tf_op jit(solution)/shard_map/ppermute | solution.py:196
  34.5 1.9 %collective-permute-start.6 = (bf16[8,112,128]{2,1,0:T(8,128)(2,1)S(1)}, bf16[8,112,128]{2,1,0:T(8,128)(2,1)S(1)}, u32[]{:S(2)}, u32[]{:S(2)}) collective-permute-start(bf16[8,112,128]{2,1,0:T(8,128)(2,1)S(1)} %get-tuple-element.7), channel_id=1, source_target_pairs={{0,128},{128,256},{256,384},{384,0},{1,129},{129,257},{257,385},{3... | collective-permute-start | bytes 688136 | tf_op jit(solution)/shard_map/ppermute | solution.py:244
  36.4 3.9 %collective-permute-start.7 = (bf16[8,112,128]{2,1,0:T(8,128)(2,1)S(1)}, bf16[8,112,128]{2,1,0:T(8,128)(2,1)S(1)}, u32[]{:S(2)}, u32[]{:S(2)}) collective-permute-start(bf16[8,112,128]{2,1,0:T(8,128)(2,1)S(1)} %get-tuple-element.8), channel_id=1, source_target_pairs={{128,0},{256,128},{384,256},{0,384},{129,1},{257,129},{385,257},{1... | collective-permute-start | bytes 688136 | tf_op jit(solution)/shard_map/ppermute | solution.py:245
  40.3 0.0 collective-permute-done.3
  40.4 8.2 %collective-permute-start.4 = (bf16[4,32,512]{2,1,0:T(8,128)(2,1)S(1)}, bf16[4,32,512]{2,1,0:T(8,128)(2,1)S(1)}, u32[]{:S(2)}, u32[]{:S(2)}) collective-permute-start(bf16[4,32,512]{2,1,0:T(8,128)(2,1)S(1)} %constant_dynamic-slice_fusion.1), channel_id=1, source_target_pairs={{0,8},{8,0},{1,9},{9,1},{2,10},{10,2},{3,11},{11,3},{4,12},{12,4},... | collective-permute-start | bytes 393224 | tf_op jit(solution)/shard_map/ppermute | solution.py:196
  48.6 0.1 copy.15
  48.8 0.1 reshape.17.weight_ref
  48.9 2.0 %shard_map.48.toep_ref = bf16[16,56,256]{2,1,0:T(8,128)(2,1)S(1)} custom-call(f32[16,256]{1,0:T(8,128)S(1)} %pad_convert_fusion.taps_ref), custom_call_target="tpu_custom_call" | custom-call | flops 10000000 | bytes 1000000 | tf_op jit(solution)/shard_map/pallas_call | solution.py:235
  50.9 0.0 collective-permute-done.7.high_ref
  50.9 1.5 %shard_map.49.zonal = f32[3584,128]{1,0:T(8,128)S(1)} custom-call(bf16[8,112,128]{2,1,0:T(8,128)(2,1)S(1)} %collective-permute-done.6.low_ref, bf16[8,8,48,128]{3,2,1,0:T(8,128)(2,1)S(1)} %all-to-all-done.run_ref.mid_ref, bf16[8,112,128]{2,1,0:T(8,128)(2,1)S(1)} %collective-permute-done.7.high_ref, bf16[16,56,256]{2,1,0:T(8,128)(2,1)S(1)} %shard_map.48.toep_ref), custom_call_target="tpu_custom_call" | custom-call | flops 1000000000 | bytes 3000000 | tf_op jit(solution)/shard_map/pallas_call | solution.py:248
  52.4 0.6 collective-permute-done.4.unused_ref
  53.0 4.2 %shard_map.50 = bf16[32,6,16,128]{3,2,1,0:T(8,128)(2,1)} custom-call(bf16[4,32,512]{2,1,0:T(8,128)(2,1)S(1)} %collective-permute-done.4.unused_ref, f32[3584,128]{1,0:T(8,128)S(1)} %shard_map.49.zonal, bf16[16,144]{1,0:T(8,128)(2,1)S(1)} %reshape.17.weight_ref), custom_call_target="tpu_custom_call" | custom-call | flops 1000000000 | bytes 3000000 | tf_op jit(solution)/shard_map/pallas_call | solution.py:251
  57.2 10.6 %all-to-all-start.1 = ((bf16[32,6,16,128]{3,2,1,0:T(8,128)(2,1)}), bf16[32,6,16,128]{3,2,1,0:T(8,128)(2,1)S(1)}, u32[]{:S(2)}, u32[]{:S(2)}) async-start(bf16[32,6,16,128]{3,2,1,0:T(8,128)(2,1)} %shard_map.50), calls=%async_computation.1 | async-start | bytes 1572864 | tf_op jit(solution)/shard_map/all_to_all | solution.py:258
  67.9 2.2 %collective-permute-start.5 = (bf16[4,32,512]{2,1,0:T(8,128)(2,1)S(1)}, bf16[4,32,512]{2,1,0:T(8,128)(2,1)S(1)}, u32[]{:S(2)}, u32[]{:S(2)}) collective-permute-start(bf16[4,32,512]{2,1,0:T(8,128)(2,1)S(1)} %collective-permute-done.4.unused_ref), channel_id=1, source_target_pairs={{0,16},{16,0},{1,17},{17,1},{2,18},{18,2},{3,19},{19,3},{4,20},{20... | collective-permute-start | bytes 393224 | tf_op jit(solution)/shard_map/ppermute | solution.py:196
  70.1 1.0 collective-permute-done.5
  71.1 0.0 copy-start.2
  71.1 22.5 %all-to-all-done.1.hidden_ref = bf16[32,6,16,128]{3,2,1,0:T(8,128)(2,1)S(1)} async-done(((bf16[32,6,16,128]{3,2,1,0:T(8,128)(2,1)}), bf16[32,6,16,128]{3,2,1,0:T(8,128)(2,1)S(1)}, u32[]{:S(2)}, u32[]{:S(2)}) %all-to-all-start.1) | async-done | bytes 786464 | tf_op jit(solution)/shard_map/all_to_all | solution.py:258
  93.7 1.2 shard_map.51
  94.9 30.0 %all_to_all.15 = bf16[64,3,16,128]{3,2,1,0:T(8,128)(2,1)S(1)} all-to-all(bf16[64,3,16,128]{3,2,1,0:T(8,128)(2,1)S(1)} %bitcast.11), channel_id=1, replica_groups=mesh['x'=4,'zl'=4,'core'=2,'zh'=2,'y'=8] {'zl','zh','y'}, dimensions={0} | all-to-all | bytes 1572864 | tf_op jit(solution)/shard_map/all_to_all | solution.py:265
  124.9 1.3 shard_map.52
  (25 shorter events, 0.2 us)
Async XLA Ops:
  0.0 17.9 %copy-start = (bf16[32,16,3,3]{0,1,3,2:T(8,128)(2,1)S(1)}, bf16[32,16,3,3]{0,1,3,2:T(8,128)(2,1)}, u32[]{:S(2)}) copy-start(bf16[32,16,3,3]{0,1,3,2:T(8,128)(2,1)} %param.6) | copy-start | bytes 27652
  0.0 1.1 copy-start.1
  1.1 9.3 %copy-start.3 = (bf16[32,512]{1,0:T(8,128)(2,1)S(1)}, bf16[32,512]{1,0:T(8,128)(2,1)}, u32[]{:S(2)}) copy-start(bf16[32,512]{1,0:T(8,128)(2,1)} %param.7) | copy-start | bytes 98308
  1.1 16.9 %copy-start.4 = (bf16[32,181]{1,0:T(8,128)(2,1)S(1)}, bf16[32,181]{1,0:T(8,128)(2,1)}, u32[]{:S(2)}) copy-start(bf16[32,181]{1,0:T(8,128)(2,1)} %param.5) | copy-start | bytes 34756
  3.1 31.3 %all-to-all-start = ((bf16[8,8,48,128]{3,2,1,0:T(8,128)(2,1)}), bf16[8,8,48,128]{3,2,1,0:T(8,128)(2,1)S(1)}, u32[]{:S(2)}, u32[]{:S(2)}) async-start(bf16[8,8,48,128]{3,2,1,0:T(8,128)(2,1)} %bitcast.4), calls=%async_computation | async-start | bytes 1572864 | tf_op jit(solution)/shard_map/all_to_all | solution.py:230
  10.6 7.4 %collective-permute-start.1 = (bf16[1,32,512]{2,1,0:T(8,128)(2,1)S(1)}, bf16[1,32,512]{2,1,0:T(8,128)(2,1)S(1)}, u32[]{:S(2)}, u32[]{:S(2)}) collective-permute-start(bf16[1,32,512]{2,1,0:T(8,128)(2,1)S(1)} %copy.9), channel_id=1, source_target_pairs={{0,7},{1,0},{2,1},{3,2},{4,3},{5,4},{6,5},{7,6},{8,15},{9,8},{10,9... | collective-permute-start | bytes 98312 | tf_op jit(solution)/shard_map/ppermute | solution.py:196
  16.0 7.0 %collective-permute-start = (bf16[1,32,512]{2,1,0:T(8,128)(2,1)S(1)}, bf16[1,32,512]{2,1,0:T(8,128)(2,1)S(1)}, u32[]{:S(2)}, u32[]{:S(2)}) collective-permute-start(bf16[1,32,512]{2,1,0:T(8,128)(2,1)S(1)} %copy.9), channel_id=1, source_target_pairs={{0,1},{1,2},{2,3},{3,4},{4,5},{5,6},{6,7},{7,0},{8,9},{9,10},{10,1... | collective-permute-start | bytes 98312 | tf_op jit(solution)/shard_map/ppermute | solution.py:196
  23.0 11.3 %collective-permute-start.2 = (bf16[3,32,512]{2,1,0:T(8,128)(2,1)S(1)}, bf16[3,32,512]{2,1,0:T(8,128)(2,1)S(1)}, u32[]{:S(2)}, u32[]{:S(2)}) collective-permute-start(bf16[3,32,512]{2,1,0:T(8,128)(2,1)S(1)} %pad_maximum_fusion), channel_id=1, source_target_pairs={{0,3},{1,4},{2,5},{3,6},{4,7},{5,0},{6,1},{7,2},{8,11},{9,12},{10,... | collective-permute-start | bytes 294920 | tf_op jit(solution)/shard_map/ppermute | solution.py:196
  25.0 15.4 %collective-permute-start.3 = (bf16[2,32,512]{2,1,0:T(8,128)(2,1)S(1)}, bf16[2,32,512]{2,1,0:T(8,128)(2,1)S(1)}, u32[]{:S(2)}, u32[]{:S(2)}) collective-permute-start(bf16[2,32,512]{2,1,0:T(8,128)(2,1)S(1)} %pad_maximum_fusion.1), channel_id=1, source_target_pairs={{0,5},{1,6},{2,7},{3,0},{4,1},{5,2},{6,3},{7,4},{8,13},{9,14},{10,... | collective-permute-start | bytes 196616 | tf_op jit(solution)/shard_map/ppermute | solution.py:196
  34.5 16.4 %collective-permute-start.6 = (bf16[8,112,128]{2,1,0:T(8,128)(2,1)S(1)}, bf16[8,112,128]{2,1,0:T(8,128)(2,1)S(1)}, u32[]{:S(2)}, u32[]{:S(2)}) collective-permute-start(bf16[8,112,128]{2,1,0:T(8,128)(2,1)S(1)} %get-tuple-element.7), channel_id=1, source_target_pairs={{0,128},{128,256},{256,384},{384,0},{1,129},{129,257},{257,385},{3... | collective-permute-start | bytes 688136 | tf_op jit(solution)/shard_map/ppermute | solution.py:244
  36.4 14.4 %collective-permute-start.7 = (bf16[8,112,128]{2,1,0:T(8,128)(2,1)S(1)}, bf16[8,112,128]{2,1,0:T(8,128)(2,1)S(1)}, u32[]{:S(2)}, u32[]{:S(2)}) collective-permute-start(bf16[8,112,128]{2,1,0:T(8,128)(2,1)S(1)} %get-tuple-element.8), channel_id=1, source_target_pairs={{128,0},{256,128},{384,256},{0,384},{129,1},{257,129},{385,257},{1... | collective-permute-start | bytes 688136 | tf_op jit(solution)/shard_map/ppermute | solution.py:245
  40.4 12.6 %collective-permute-start.4 = (bf16[4,32,512]{2,1,0:T(8,128)(2,1)S(1)}, bf16[4,32,512]{2,1,0:T(8,128)(2,1)S(1)}, u32[]{:S(2)}, u32[]{:S(2)}) collective-permute-start(bf16[4,32,512]{2,1,0:T(8,128)(2,1)S(1)} %constant_dynamic-slice_fusion.1), channel_id=1, source_target_pairs={{0,8},{8,0},{1,9},{9,1},{2,10},{10,2},{3,11},{11,3},{4,12},{12,4},... | collective-permute-start | bytes 393224 | tf_op jit(solution)/shard_map/ppermute | solution.py:196
  57.2 36.5 %all-to-all-start.1 = ((bf16[32,6,16,128]{3,2,1,0:T(8,128)(2,1)}), bf16[32,6,16,128]{3,2,1,0:T(8,128)(2,1)S(1)}, u32[]{:S(2)}, u32[]{:S(2)}) async-start(bf16[32,6,16,128]{3,2,1,0:T(8,128)(2,1)} %shard_map.50), calls=%async_computation.1 | async-start | bytes 1572864 | tf_op jit(solution)/shard_map/all_to_all | solution.py:258
  67.9 3.2 %collective-permute-start.5 = (bf16[4,32,512]{2,1,0:T(8,128)(2,1)S(1)}, bf16[4,32,512]{2,1,0:T(8,128)(2,1)S(1)}, u32[]{:S(2)}, u32[]{:S(2)}) collective-permute-start(bf16[4,32,512]{2,1,0:T(8,128)(2,1)S(1)} %collective-permute-done.4.unused_ref), channel_id=1, source_target_pairs={{0,16},{16,0},{1,17},{17,1},{2,18},{18,2},{3,19},{19,3},{4,20},{20... | collective-permute-start | bytes 393224 | tf_op jit(solution)/shard_map/ppermute | solution.py:196
  71.1 53.8 %copy-start.2 = (bf16[2,32,45,128]{3,1,2,0:T(8,128)(2,1)S(1)}, bf16[2,32,45,128]{3,1,2,0:T(8,128)(2,1)}, u32[]{:S(2)}) copy-start(bf16[2,32,45,128]{3,1,2,0:T(8,128)(2,1)} %param.4) | copy-start | bytes 2211844

commit v5 on v3

--- a/solution.py
+++ b/solution.py
@@ -57,7 +57,7 @@
     return jnp.concatenate([v[:, 64:], v[:, :64]], axis=1)
 
 
-def rim_kernel(run_ref, low_ref, high_ref):
+def rim_kernel(run_ref, unused_ref, low_ref, high_ref):
     low_ref[:, 0:16] = run_ref[5, :, 32:48]
     low_ref[:, 16:64] = run_ref[6]
     low_ref[:, 64:112] = run_ref[7]
@@ -238,7 +238,7 @@
     east = [(i, (i + 1) % count) for i in range(count)]
     west = [(b, a) for a, b in east]
     rim = jax.ShapeDtypeStruct((8, 112, 128), BF16)
-    low, high = kernel_call(rim_kernel, [rim, rim], cost=(0, 10**6))(run)
+    low, high = kernel_call(rim_kernel, [rim, rim], in_specs=[vmem, loose], cost=(0, 10**6))(run, toeplitz)
     low = lax.ppermute(low, "x", east)
     high = lax.ppermute(high, "x", west)
 

time: 129 us -> 129 us (level)
  no operation moved by 1% of the time
where the time goes in v5:
time: 129 us; the launch traced here: 126 us
  starting transfers between devices  50 us (39%)
  waiting for transfers between devices  31.1 us (24%)
  blocking collectives  30.7 us (24%)
  Pallas kernels  12.2 us (9%)
  local copies, waits for them, and re-layouts  1.74 us (1%)
    all_to_all x1, blocking collectives, per_device(): lax.all_to_all(mixed.reshape(64, 3, GROUP, 128), ('zl', 'zh', 'y'), 0, 0,...  30.7 us
    ppermute x6, starting transfers between devices, from_behind(): lax.ppermute(blocks, axis, [(i, (i + step) % count) for i in range(count)])  26.6 us
    all_to_all x1, waiting for transfers between devices, per_device(): gathered = lax.all_to_all(hidden, ('core', 'zh', 'y'), 0, 0, tiled=True)  22.7 us
    all_to_all x1, starting transfers between devices, per_device(): gathered = lax.all_to_all(hidden, ('core', 'zh', 'y'), 0, 0, tiled=True)  10.4 us
    ppermute x6, waiting for transfers between devices, from_behind(): lax.ppermute(blocks, axis, [(i, (i + step) % count) for i in range(count)])  8.42 us
    all_to_all x1, starting transfers between devices, per_device(): lax.all_to_all(units.reshape(BLOCKS, 8, SLOT, 128), ('zl', 'core'), 0, 0,...  7.27 us
    pallas_call x1, Pallas kernels, per_device(): kernel_call(conv_kernel, (32, 6, GROUP, 128), scratch=(pltpu.VMEM((4, 3,...  4.23 us
    ppermute x1, starting transfers between devices, per_device(): high = lax.ppermute(high, 'x', west)  3.58 us
  transfers between devices with their start and end apart: 10, of which 5 were waited for; matrix products, arithmetic and copies ran while one was open for 1% of the time, Pallas kernels for 3%

profile of v5, /device:TPU:6, one launch (start us, length us, event | category | flops | bytes accessed | tf_op | source)
XLA Modules:
  0.0 126.2 jit_solution(16215256121771916581)
XLA Ops:
  0.0 1.1 copy-done.1
  1.1 2.0 %shard_map.46 = bf16[2,2,2,8,48,128]{5,4,3,2,1,0:T(8,128)(2,1)} custom-call(bf16[2,45,32,128]{3,2,1,0:T(8,128)(2,1)S(1)} %bitcast.13), custom_call_target="tpu_custom_call" | custom-call | flops 200000000 | bytes 3000000 | tf_op jit(solution)/shard_map/pallas_call | solution.py:222
  3.1 7.3 %all-to-all-start = ((bf16[8,8,48,128]{3,2,1,0:T(8,128)(2,1)}), bf16[8,8,48,128]{3,2,1,0:T(8,128)(2,1)S(1)}, u32[]{:S(2)}, u32[]{:S(2)}) async-start(bf16[8,8,48,128]{3,2,1,0:T(8,128)(2,1)} %bitcast.4), calls=%async_computation | async-start | bytes 1572864 | tf_op jit(solution)/shard_map/all_to_all | solution.py:228
  10.4 0.1 copy.7
  10.5 0.1 copy.9
  10.6 5.4 %collective-permute-start.1 = (bf16[1,32,512]{2,1,0:T(8,128)(2,1)S(1)}, bf16[1,32,512]{2,1,0:T(8,128)(2,1)S(1)}, u32[]{:S(2)}, u32[]{:S(2)}) collective-permute-start(bf16[1,32,512]{2,1,0:T(8,128)(2,1)S(1)} %copy.9), channel_id=1, source_target_pairs={{0,7},{1,0},{2,1},{3,2},{4,3},{5,4},{6,5},{7,6},{8,15},{9,8},{10,9... | collective-permute-start | bytes 98312 | tf_op jit(solution)/shard_map/ppermute | solution.py:197
  16.0 1.9 %collective-permute-start = (bf16[1,32,512]{2,1,0:T(8,128)(2,1)S(1)}, bf16[1,32,512]{2,1,0:T(8,128)(2,1)S(1)}, u32[]{:S(2)}, u32[]{:S(2)}) collective-permute-start(bf16[1,32,512]{2,1,0:T(8,128)(2,1)S(1)} %copy.9), channel_id=1, source_target_pairs={{0,1},{1,2},{2,3},{3,4},{4,5},{5,6},{6,7},{7,0},{8,9},{9,10},{10,1... | collective-permute-start | bytes 98312 | tf_op jit(solution)/shard_map/ppermute | solution.py:197
  18.0 2.0 %shard_map.47.unused_ref.toep_ref = bf16[16,56,256]{2,1,0:T(8,128)(2,1)S(1)} custom-call(f32[16,256]{1,0:T(8,128)S(1)} %pad_convert_fusion.taps_ref), custom_call_target="tpu_custom_call" | custom-call | flops 10000000 | bytes 1000000 | tf_op jit(solution)/shard_map/pallas_call | solution.py:233
  20.0 0.0 collective-permute-done.1
  20.0 3.0 %collective-permute-done = bf16[1,32,512]{2,1,0:T(8,128)(2,1)S(1)} collective-permute-done((bf16[1,32,512]{2,1,0:T(8,128)(2,1)S(1)}, bf16[1,32,512]{2,1,0:T(8,128)(2,1)S(1)}, u32[]{:S(2)}, u32[]{:S(2)}) %collective-permute-start) | collective-permute-done | bytes 32800 | tf_op jit(solution)/shard_map/ppermute | solution.py:197
  23.0 2.2 %collective-permute-start.2 = (bf16[3,32,512]{2,1,0:T(8,128)(2,1)S(1)}, bf16[3,32,512]{2,1,0:T(8,128)(2,1)S(1)}, u32[]{:S(2)}, u32[]{:S(2)}) collective-permute-start(bf16[3,32,512]{2,1,0:T(8,128)(2,1)S(1)} %pad_maximum_fusion), channel_id=1, source_target_pairs={{0,3},{1,4},{2,5},{3,6},{4,7},{5,0},{6,1},{7,2},{8,11},{9,12},{10,... | collective-permute-start | bytes 294920 | tf_op jit(solution)/shard_map/ppermute | solution.py:197
  25.3 6.6 %collective-permute-start.3 = (bf16[2,32,512]{2,1,0:T(8,128)(2,1)S(1)}, bf16[2,32,512]{2,1,0:T(8,128)(2,1)S(1)}, u32[]{:S(2)}, u32[]{:S(2)}) collective-permute-start(bf16[2,32,512]{2,1,0:T(8,128)(2,1)S(1)} %pad_maximum_fusion.1), channel_id=1, source_target_pairs={{0,5},{1,6},{2,7},{3,0},{4,1},{5,2},{6,3},{7,4},{8,13},{9,14},{10,... | collective-permute-start | bytes 196616 | tf_op jit(solution)/shard_map/ppermute | solution.py:197
  31.9 2.4 %collective-permute-done.2 = bf16[3,32,512]{2,1,0:T(8,128)(2,1)S(1)} collective-permute-done((bf16[3,32,512]{2,1,0:T(8,128)(2,1)S(1)}, bf16[3,32,512]{2,1,0:T(8,128)(2,1)S(1)}, u32[]{:S(2)}, u32[]{:S(2)}) %collective-permute-start.2) | collective-permute-done | bytes 98336 | tf_op jit(solution)/shard_map/ppermute | solution.py:197
  34.4 0.0 all-to-all-done.run_ref.mid_ref
  34.4 2.3 %collective-permute-start.6 = (bf16[8,112,128]{2,1,0:T(8,128)(2,1)S(1)}, bf16[8,112,128]{2,1,0:T(8,128)(2,1)S(1)}, u32[]{:S(2)}, u32[]{:S(2)}) collective-permute-start(bf16[8,112,128]{2,1,0:T(8,128)(2,1)S(1)} %get-tuple-element.7), channel_id=1, source_target_pairs={{0,128},{128,256},{256,384},{384,0},{1,129},{129,257},{257,385},{3... | collective-permute-start | bytes 688136 | tf_op jit(solution)/shard_map/ppermute | solution.py:242
  36.7 3.6 %collective-permute-start.7 = (bf16[8,112,128]{2,1,0:T(8,128)(2,1)S(1)}, bf16[8,112,128]{2,1,0:T(8,128)(2,1)S(1)}, u32[]{:S(2)}, u32[]{:S(2)}) collective-permute-start(bf16[8,112,128]{2,1,0:T(8,128)(2,1)S(1)} %get-tuple-element.8), channel_id=1, source_target_pairs={{128,0},{256,128},{384,256},{0,384},{129,1},{257,129},{385,257},{1... | collective-permute-start | bytes 688136 | tf_op jit(solution)/shard_map/ppermute | solution.py:243
  40.3 8.2 %collective-permute-start.4 = (bf16[4,32,512]{2,1,0:T(8,128)(2,1)S(1)}, bf16[4,32,512]{2,1,0:T(8,128)(2,1)S(1)}, u32[]{:S(2)}, u32[]{:S(2)}) collective-permute-start(bf16[4,32,512]{2,1,0:T(8,128)(2,1)S(1)} %constant_dynamic-slice_fusion.1), channel_id=1, source_target_pairs={{0,8},{8,0},{1,9},{9,1},{2,10},{10,2},{3,11},{11,3},{4,12},{12,4},... | collective-permute-start | bytes 393224 | tf_op jit(solution)/shard_map/ppermute | solution.py:197
  48.6 0.1 dynamic-slice_bitcast_fusion
  48.6 0.1 copy.15
  48.8 0.1 reshape.17.weight_ref
  48.9 0.0 collective-permute-done.6.low_ref
  48.9 1.5 %shard_map.49.zonal = f32[3584,128]{1,0:T(8,128)S(1)} custom-call(bf16[8,112,128]{2,1,0:T(8,128)(2,1)S(1)} %collective-permute-done.6.low_ref, bf16[8,8,48,128]{3,2,1,0:T(8,128)(2,1)S(1)} %all-to-all-done.run_ref.mid_ref, bf16[8,112,128]{2,1,0:T(8,128)(2,1)S(1)} %collective-permute-done.7.high_ref, bf16[16,56,256]{2,1,0:T(8,128)(2,1)S(1)} %shard_map.47.unused_ref.toep_ref), custom_call_target="tpu_custom_call" | custom-call | flops 1000000000 | bytes 3000000 | tf_op jit(solution)/shard_map/pallas_call | solution.py:246
  50.4 2.0 %collective-permute-done.4.unused_ref = bf16[4,32,512]{2,1,0:T(8,128)(2,1)S(1)} collective-permute-done((bf16[4,32,512]{2,1,0:T(8,128)(2,1)S(1)}, bf16[4,32,512]{2,1,0:T(8,128)(2,1)S(1)}, u32[]{:S(2)}, u32[]{:S(2)}) %collective-permute-start.4) | collective-permute-done | bytes 131104 | tf_op jit(solution)/shard_map/ppermute | solution.py:197
  52.4 4.2 %shard_map.50 = bf16[32,6,16,128]{3,2,1,0:T(8,128)(2,1)} custom-call(bf16[4,32,512]{2,1,0:T(8,128)(2,1)S(1)} %collective-permute-done.4.unused_ref, f32[3584,128]{1,0:T(8,128)S(1)} %shard_map.49.zonal, bf16[16,144]{1,0:T(8,128)(2,1)S(1)} %reshape.17.weight_ref), custom_call_target="tpu_custom_call" | custom-call | flops 1000000000 | bytes 3000000 | tf_op jit(solution)/shard_map/pallas_call | solution.py:249
  56.6 10.4 %all-to-all-start.1 = ((bf16[32,6,16,128]{3,2,1,0:T(8,128)(2,1)}), bf16[32,6,16,128]{3,2,1,0:T(8,128)(2,1)S(1)}, u32[]{:S(2)}, u32[]{:S(2)}) async-start(bf16[32,6,16,128]{3,2,1,0:T(8,128)(2,1)} %shard_map.50), calls=%async_computation.1 | async-start | bytes 1572864 | tf_op jit(solution)/shard_map/all_to_all | solution.py:256
  67.0 2.2 %collective-permute-start.5 = (bf16[4,32,512]{2,1,0:T(8,128)(2,1)S(1)}, bf16[4,32,512]{2,1,0:T(8,128)(2,1)S(1)}, u32[]{:S(2)}, u32[]{:S(2)}) collective-permute-start(bf16[4,32,512]{2,1,0:T(8,128)(2,1)S(1)} %collective-permute-done.4.unused_ref), channel_id=1, source_target_pairs={{0,16},{16,0},{1,17},{17,1},{2,18},{18,2},{3,19},{19,3},{4,20},{20... | collective-permute-start | bytes 393224 | tf_op jit(solution)/shard_map/ppermute | solution.py:197
  69.3 1.0 collective-permute-done.5
  70.3 0.0 copy-start.2
  70.3 22.7 %all-to-all-done.1.hidden_ref = bf16[32,6,16,128]{3,2,1,0:T(8,128)(2,1)S(1)} async-done(((bf16[32,6,16,128]{3,2,1,0:T(8,128)(2,1)}), bf16[32,6,16,128]{3,2,1,0:T(8,128)(2,1)S(1)}, u32[]{:S(2)}, u32[]{:S(2)}) %all-to-all-start.1) | async-done | bytes 786464 | tf_op jit(solution)/shard_map/all_to_all | solution.py:256
  92.9 1.2 shard_map.51
  94.2 30.7 %all_to_all.15 = bf16[64,3,16,128]{3,2,1,0:T(8,128)(2,1)S(1)} all-to-all(bf16[64,3,16,128]{3,2,1,0:T(8,128)(2,1)S(1)} %bitcast.11), channel_id=1, replica_groups=mesh['x'=4,'zl'=4,'core'=2,'zh'=2,'y'=8] {'zl','zh','y'}, dimensions={0} | all-to-all | bytes 1572864 | tf_op jit(solution)/shard_map/all_to_all | solution.py:263
  124.9 1.3 %shard_map.52 = bf16[2,45,32,128]{3,2,1,0:T(8,128)(2,1)} custom-call(bf16[2,2,48,16,128]{4,3,2,1,0:T(8,128)(2,1)S(1)} %bitcast.12, bf16[2,45,32,128]{3,2,1,0:T(8,128)(2,1)S(1)} %bitcast.14), custom_call_target="tpu_custom_call" | custom-call | flops 200000000 | bytes 3000000 | tf_op jit(solution)/shard_map/pallas_call | solution.py:264
  (25 shorter events, 0.2 us)
Async XLA Ops:
  0.0 48.5 %copy-start = (bf16[32,16,3,3]{0,1,3,2:T(8,128)(2,1)S(1)}, bf16[32,16,3,3]{0,1,3,2:T(8,128)(2,1)}, u32[]{:S(2)}) copy-start(bf16[32,16,3,3]{0,1,3,2:T(8,128)(2,1)} %param.6) | copy-start | bytes 27652
  0.0 1.1 copy-start.1
  1.1 9.3 %copy-start.3 = (bf16[32,512]{1,0:T(8,128)(2,1)S(1)}, bf16[32,512]{1,0:T(8,128)(2,1)}, u32[]{:S(2)}) copy-start(bf16[32,512]{1,0:T(8,128)(2,1)} %param.7) | copy-start | bytes 98308
  1.1 16.8 %copy-start.4 = (bf16[32,181]{1,0:T(8,128)(2,1)S(1)}, bf16[32,181]{1,0:T(8,128)(2,1)}, u32[]{:S(2)}) copy-start(bf16[32,181]{1,0:T(8,128)(2,1)} %param.5) | copy-start | bytes 34756
  3.1 31.2 %all-to-all-start = ((bf16[8,8,48,128]{3,2,1,0:T(8,128)(2,1)}), bf16[8,8,48,128]{3,2,1,0:T(8,128)(2,1)S(1)}, u32[]{:S(2)}, u32[]{:S(2)}) async-start(bf16[8,8,48,128]{3,2,1,0:T(8,128)(2,1)} %bitcast.4), calls=%async_computation | async-start | bytes 1572864 | tf_op jit(solution)/shard_map/all_to_all | solution.py:228
  10.6 9.4 %collective-permute-start.1 = (bf16[1,32,512]{2,1,0:T(8,128)(2,1)S(1)}, bf16[1,32,512]{2,1,0:T(8,128)(2,1)S(1)}, u32[]{:S(2)}, u32[]{:S(2)}) collective-permute-start(bf16[1,32,512]{2,1,0:T(8,128)(2,1)S(1)} %copy.9), channel_id=1, source_target_pairs={{0,7},{1,0},{2,1},{3,2},{4,3},{5,4},{6,5},{7,6},{8,15},{9,8},{10,9... | collective-permute-start | bytes 98312 | tf_op jit(solution)/shard_map/ppermute | solution.py:197
  16.0 7.0 %collective-permute-start = (bf16[1,32,512]{2,1,0:T(8,128)(2,1)S(1)}, bf16[1,32,512]{2,1,0:T(8,128)(2,1)S(1)}, u32[]{:S(2)}, u32[]{:S(2)}) collective-permute-start(bf16[1,32,512]{2,1,0:T(8,128)(2,1)S(1)} %copy.9), channel_id=1, source_target_pairs={{0,1},{1,2},{2,3},{3,4},{4,5},{5,6},{6,7},{7,0},{8,9},{9,10},{10,1... | collective-permute-start | bytes 98312 | tf_op jit(solution)/shard_map/ppermute | solution.py:197
  23.0 11.2 %collective-permute-start.2 = (bf16[3,32,512]{2,1,0:T(8,128)(2,1)S(1)}, bf16[3,32,512]{2,1,0:T(8,128)(2,1)S(1)}, u32[]{:S(2)}, u32[]{:S(2)}) collective-permute-start(bf16[3,32,512]{2,1,0:T(8,128)(2,1)S(1)} %pad_maximum_fusion), channel_id=1, source_target_pairs={{0,3},{1,4},{2,5},{3,6},{4,7},{5,0},{6,1},{7,2},{8,11},{9,12},{10,... | collective-permute-start | bytes 294920 | tf_op jit(solution)/shard_map/ppermute | solution.py:197
  25.3 14.9 %collective-permute-start.3 = (bf16[2,32,512]{2,1,0:T(8,128)(2,1)S(1)}, bf16[2,32,512]{2,1,0:T(8,128)(2,1)S(1)}, u32[]{:S(2)}, u32[]{:S(2)}) collective-permute-start(bf16[2,32,512]{2,1,0:T(8,128)(2,1)S(1)} %pad_maximum_fusion.1), channel_id=1, source_target_pairs={{0,5},{1,6},{2,7},{3,0},{4,1},{5,2},{6,3},{7,4},{8,13},{9,14},{10,... | collective-permute-start | bytes 196616 | tf_op jit(solution)/shard_map/ppermute | solution.py:197
  34.4 14.5 %collective-permute-start.6 = (bf16[8,112,128]{2,1,0:T(8,128)(2,1)S(1)}, bf16[8,112,128]{2,1,0:T(8,128)(2,1)S(1)}, u32[]{:S(2)}, u32[]{:S(2)}) collective-permute-start(bf16[8,112,128]{2,1,0:T(8,128)(2,1)S(1)} %get-tuple-element.7), channel_id=1, source_target_pairs={{0,128},{128,256},{256,384},{384,0},{1,129},{129,257},{257,385},{3... | collective-permute-start | bytes 688136 | tf_op jit(solution)/shard_map/ppermute | solution.py:242
  36.7 12.2 %collective-permute-start.7 = (bf16[8,112,128]{2,1,0:T(8,128)(2,1)S(1)}, bf16[8,112,128]{2,1,0:T(8,128)(2,1)S(1)}, u32[]{:S(2)}, u32[]{:S(2)}) collective-permute-start(bf16[8,112,128]{2,1,0:T(8,128)(2,1)S(1)} %get-tuple-element.8), channel_id=1, source_target_pairs={{128,0},{256,128},{384,256},{0,384},{129,1},{257,129},{385,257},{1... | collective-permute-start | bytes 688136 | tf_op jit(solution)/shard_map/ppermute | solution.py:243
  40.3 12.1 %collective-permute-start.4 = (bf16[4,32,512]{2,1,0:T(8,128)(2,1)S(1)}, bf16[4,32,512]{2,1,0:T(8,128)(2,1)S(1)}, u32[]{:S(2)}, u32[]{:S(2)}) collective-permute-start(bf16[4,32,512]{2,1,0:T(8,128)(2,1)S(1)} %constant_dynamic-slice_fusion.1), channel_id=1, source_target_pairs={{0,8},{8,0},{1,9},{9,1},{2,10},{10,2},{3,11},{11,3},{4,12},{12,4},... | collective-permute-start | bytes 393224 | tf_op jit(solution)/shard_map/ppermute | solution.py:197
  56.6 36.3 %all-to-all-start.1 = ((bf16[32,6,16,128]{3,2,1,0:T(8,128)(2,1)}), bf16[32,6,16,128]{3,2,1,0:T(8,128)(2,1)S(1)}, u32[]{:S(2)}, u32[]{:S(2)}) async-start(bf16[32,6,16,128]{3,2,1,0:T(8,128)(2,1)} %shard_map.50), calls=%async_computation.1 | async-start | bytes 1572864 | tf_op jit(solution)/shard_map/all_to_all | solution.py:256
  67.0 3.2 %collective-permute-start.5 = (bf16[4,32,512]{2,1,0:T(8,128)(2,1)S(1)}, bf16[4,32,512]{2,1,0:T(8,128)(2,1)S(1)}, u32[]{:S(2)}, u32[]{:S(2)}) collective-permute-start(bf16[4,32,512]{2,1,0:T(8,128)(2,1)S(1)} %collective-permute-done.4.unused_ref), channel_id=1, source_target_pairs={{0,16},{16,0},{1,17},{17,1},{2,18},{18,2},{3,19},{19,3},{4,20},{20... | collective-permute-start | bytes 393224 | tf_op jit(solution)/shard_map/ppermute | solution.py:197
  70.3 54.7 %copy-start.2 = (bf16[2,32,45,128]{3,1,2,0:T(8,128)(2,1)S(1)}, bf16[2,32,45,128]{3,1,2,0:T(8,128)(2,1)}, u32[]{:S(2)}) copy-start(bf16[2,32,45,128]{3,1,2,0:T(8,128)(2,1)} %param.4) | copy-start | bytes 2211844
